TPU v7x, 32 devices: a whole 2x2x4 slice. The times are simulated.
32 devices in a mesh: leaf: 8 (over z, core), blk: 4 (over y, x).
Axes of the slice: x: 2, y: 2, z: 4, core: 2. Of those that a mesh axis runs over, the one named last changes fastest.
Arguments:
- tokens: bfloat16 [16384, 512], P(('leaf', 'blk')), may hold values from -6 to 6
- cotangent: bfloat16 [16384, 512], P(('leaf', 'blk')), may hold values from -6 to 6
- encoded: bfloat16 [512, 512], P(('leaf', 'blk')), may hold values from -6 to 6
- parents: int32 [8, 16], P('leaf'), may hold values from 0 to 14, as said below
- timestep: int32 [8], P('leaf'), may hold values from 0 to 49
- w_qkv: bfloat16 [512, 1536], P(('leaf', 'blk')), may hold values from -0.375 to 0.375
- w_o: bfloat16 [512, 512], P(('leaf', 'blk')), may hold values from -1.5 to 1.5
- w_cq: bfloat16 [512, 512], P(('leaf', 'blk')), may hold values from -0.375 to 0.375
- w_ckv: bfloat16 [512, 1024], P(('leaf', 'blk')), may hold values from -0.375 to 0.375
- w_co: bfloat16 [512, 512], P(('leaf', 'blk')), may hold values from -0.5 to 0.5
- w_in: bfloat16 [512, 2048], P(('leaf', 'blk')), may hold values from -0.25 to 0.25
- w_out: bfloat16 [2048, 512], P(('leaf', 'blk')), may hold values from -0.25 to 0.25
- mod_table: bfloat16 [50, 3072], P(None, ('leaf', 'blk')), may hold values from -2 to 2
Outputs:
- mixed: bfloat16 [16384, 512], P(('leaf', 'blk'))
- grad_tokens: float32 [16384, 512], P(('leaf', 'blk'))
- grad_encoded: float32 [512, 512], P(('leaf', 'blk'))
- grad_qkv: float32 [512, 1536], P(('leaf', 'blk'))
- grad_o: float32 [512, 512], P(('leaf', 'blk'))
- grad_cq: float32 [512, 512], P(('leaf', 'blk'))
- grad_ckv: float32 [512, 1024], P(('leaf', 'blk'))
- grad_co: float32 [512, 512], P(('leaf', 'blk'))
- grad_in: float32 [512, 2048], P(('leaf', 'blk'))
- grad_out: float32 [2048, 512], P(('leaf', 'blk'))
- grad_table: float32 [50, 3072], P(None, ('leaf', 'blk'))
Inputs may be any that keep to these rules, and one draw needn't show every extreme that they name: `parents`: block 0 of each tree is its own parent; every other block's parent is an earlier block of the same tree, and the last block's parent is the block before it.
All inputs are finite; a program needn't handle non-finite values.
Results may differ from a plain program's by a relative error of at most 0.02.
The roundings to bfloat16 on the way count: a program that leaves them out, or rounds other values in their place, can miss the bound.
Values may be sent and summed in bfloat16 or wider, within the bound.
A program may use at most 192 MiB of HBM per device.

v0:
```python
import functools

import jax
import jax.numpy as jnp
from jax import lax
from jax.experimental import pallas as pl
from jax.experimental.pallas import tpu as pltpu
from jax.sharding import PartitionSpec as P

D = 512
HEADS = 8
HEAD = 64
BLOCK = 128
FF = 2048
ENC = 64
STEPS = 50


PRECISE = lax.Precision.HIGHEST
MASKED = -1e30


def ancestors(parent_row):
    count = parent_row.shape[0]
    indices = jnp.arange(count, dtype=jnp.int32)
    reach_map = (indices[:, None] == indices[None, :]).astype(jnp.float32)
    reach_map = jnp.minimum(
        reach_map + (parent_row[:, None] == indices[None, :]).astype(jnp.float32), 1.0
    )
    for rounds in range(max(1, (count - 1).bit_length())):
        reach_map = jnp.minimum(jnp.dot(reach_map, reach_map, precision=PRECISE), 1.0)
    return reach_map


def normalize(values, shift, scaling):
    centred = values - jnp.mean(values, axis=-1, keepdims=True)
    spread = jnp.mean(centred * centred, axis=-1, keepdims=True)
    return centred * lax.rsqrt(spread + 1e-05) * (1.0 + scaling) + shift


def span_link(reach_rows, span):
    return lax.dynamic_slice_in_dim(reach_rows, span * 4, 4, 1)


def span_reached(reach_rows, span):
    return jnp.max(span_link(reach_rows, span)) > 0.5


def span_mask(reach_rows, first_block, span, row_count, width):
    query_index = jnp.arange(row_count, dtype=jnp.int32)
    key_index = jnp.arange(width, dtype=jnp.int32)
    query_block = first_block + query_index // BLOCK
    key_block = span * 4 + key_index // BLOCK
    link = span_link(reach_rows, span)
    link = jnp.repeat(jnp.repeat(link, BLOCK, axis=0), BLOCK, axis=1)
    same = query_block[:, None] == key_block[None, :]
    return (link > 0.5) & (
        jnp.logical_not(same) | (key_index[None, :] % BLOCK <= query_index[:, None] % BLOCK)
    )


def scores_of(queries, key_rows, allowed):
    raw = jnp.einsum(
        "qhd,khd->hqk", queries, key_rows, preferred_element_type=jnp.float32
    ) * HEAD ** (-0.5)
    return jnp.where(allowed[None], raw, MASKED)


def split_spans(keys, values):
    width = 4 * BLOCK
    count = keys.shape[0] // width
    return (
        jnp.arange(count, dtype=jnp.int32),
        keys.reshape(count, width, HEADS, HEAD),
        values.reshape(count, width, HEADS, HEAD),
    )


def tree_forward_attention(queries, keys, values, reach_rows, first_block):
    row_count = queries.shape[0]
    width = 4 * BLOCK
    spans, key_spans, value_spans = split_spans(keys, values)

    def stats(carry, item):
        span, key_rows = item

        def stats_visit(state):
            top, total = state
            allowed = span_mask(reach_rows, first_block, span, row_count, width)
            score = scores_of(queries, key_rows, allowed)
            new_top = jnp.maximum(top, jnp.max(score, axis=-1))
            weight = jnp.where(allowed[None], jnp.exp(score - new_top[..., None]), 0.0)
            return (new_top, total * jnp.exp(top - new_top) + jnp.sum(weight, axis=-1))

        return (
            lax.cond(span_reached(reach_rows, span), stats_visit, lambda state: state, carry),
            None,
        )

    start = (
        jnp.full((HEADS, row_count), MASKED, jnp.float32),
        jnp.zeros((HEADS, row_count), jnp.float32),
    )
    (top, total), unused = lax.scan(stats, start, (spans, key_spans))
    log_total = top + jnp.log(total)

    def collect(accum, item):
        span, key_rows, value_rows = item

        def collect_visit(current):
            allowed = span_mask(reach_rows, first_block, span, row_count, width)
            weight = jnp.where(
                allowed[None],
                jnp.exp(scores_of(queries, key_rows, allowed) - log_total[..., None]),
                0.0,
            )
            return current + jnp.einsum(
                "hqk,khd->qhd",
                weight.astype(jnp.bfloat16),
                value_rows,
                preferred_element_type=jnp.float32,
            )

        return (
            lax.cond(span_reached(reach_rows, span), collect_visit, lambda current: current, accum),
            None,
        )

    attended, unused = lax.scan(
        collect, jnp.zeros((row_count, HEADS, HEAD), jnp.float32), (spans, key_spans, value_spans)
    )
    return (attended, log_total)


def tree_backward_attention(queries, keys, values, reach_rows, first_block, log_total, grad_attn):
    row_count = queries.shape[0]
    width = 4 * BLOCK
    spans, key_spans, value_spans = split_spans(keys, values)

    def probs_of(span, key_rows):
        allowed = span_mask(reach_rows, first_block, span, row_count, width)
        return jnp.where(
            allowed[None],
            jnp.exp(scores_of(queries, key_rows, allowed) - log_total[..., None]),
            0.0,
        )

    def inner_pass(total, item):
        span, key_rows, value_rows = item

        def inner_visit(current):
            weight = probs_of(span, key_rows)
            d_weight = jnp.einsum(
                "qhd,khd->hqk", grad_attn, value_rows, preferred_element_type=jnp.float32
            )
            return current + jnp.sum(weight * d_weight, axis=-1)

        return (
            lax.cond(span_reached(reach_rows, span), inner_visit, lambda current: current, total),
            None,
        )

    delta, unused = lax.scan(
        inner_pass, jnp.zeros((HEADS, row_count), jnp.float32), (spans, key_spans, value_spans)
    )

    def grad_pass(d_queries, item):
        span, key_rows, value_rows = item

        def grad_visit(current):
            weight = probs_of(span, key_rows)
            d_weight = jnp.einsum(
                "qhd,khd->hqk", grad_attn, value_rows, preferred_element_type=jnp.float32
            )
            d_score = (weight * (d_weight - delta[..., None])).astype(jnp.bfloat16)
            current = current + jnp.einsum(
                "hqk,khd->qhd", d_score, key_rows, preferred_element_type=jnp.float32
            )
            d_keys = jnp.einsum(
                "hqk,qhd->khd", d_score, queries, preferred_element_type=jnp.float32
            ) * HEAD ** (-0.5)
            d_values = jnp.einsum(
                "hqk,qhd->khd",
                weight.astype(jnp.bfloat16),
                grad_attn,
                preferred_element_type=jnp.float32,
            )
            return (
                current,
                jnp.concatenate((d_keys.reshape(width, D), d_values.reshape(width, D)), axis=1),
            )

        def skip(current):
            return (current, jnp.zeros((width, 2 * D), jnp.float32))

        return lax.cond(span_reached(reach_rows, span), grad_visit, skip, d_queries)

    d_queries, terms = lax.scan(
        grad_pass, jnp.zeros((row_count, HEADS, HEAD), jnp.float32), (spans, key_spans, value_spans)
    )
    return (d_queries * HEAD ** (-0.5), terms.reshape(-1, 2 * D))


def generic_device(
    tokens,
    cotangent,
    encoded,
    parents,
    timestep,
    w_qkv,
    w_o,
    w_cq,
    w_ckv,
    w_co,
    w_in,
    w_out,
    mod_table,
):
    gathered = (
        lax.all_gather(w_qkv, ("leaf", "blk"), axis=0, tiled=True),
        lax.all_gather(w_o, ("leaf", "blk"), axis=0, tiled=True),
        lax.all_gather(w_cq, ("leaf", "blk"), axis=0, tiled=True),
        lax.all_gather(w_ckv, ("leaf", "blk"), axis=0, tiled=True),
        lax.all_gather(w_co, ("leaf", "blk"), axis=0, tiled=True),
        lax.all_gather(w_in, ("leaf", "blk"), axis=0, tiled=True),
        lax.all_gather(w_out, ("leaf", "blk"), axis=0, tiled=True),
        lax.all_gather(mod_table, ("leaf", "blk"), axis=1, tiled=True),
    )
    g_qkv, g_o, g_cq, g_ckv, g_co, g_in, g_out, g_table = gathered
    select = (jnp.arange(STEPS, dtype=jnp.int32) == timestep[0]).astype(jnp.float32)
    modulate = jnp.dot(
        select.astype(jnp.bfloat16)[None, :], g_table, preferred_element_type=jnp.float32
    )[0]
    pieces = [modulate[i * D : (i + 1) * D] for i in range(6)]
    inputs = tokens.astype(jnp.float32)
    row_count = tokens.shape[0]
    local_blocks = row_count // BLOCK
    first_block = lax.axis_index("blk") * local_blocks
    reach_map = ancestors(parents[0])
    reach_rows = lax.dynamic_slice_in_dim(reach_map, first_block, local_blocks, 0)
    scaling = HEAD ** (-0.5)
    normed_one, pull_one = jax.vjp(normalize, inputs, pieces[0], pieces[1])
    h_first = normed_one.astype(jnp.bfloat16)
    projected = jnp.dot(h_first, g_qkv, preferred_element_type=jnp.float32).astype(jnp.bfloat16)
    queries = projected[:, :D].reshape(row_count, HEADS, HEAD)
    keys, values = (
        lax.all_gather(projected[:, D : 2 * D], "blk", axis=0, tiled=True),
        lax.all_gather(projected[:, 2 * D :], "blk", axis=0, tiled=True),
    )
    attended, log_total = tree_forward_attention(queries, keys, values, reach_rows, first_block)
    attn_low = attended.reshape(row_count, D).astype(jnp.bfloat16)
    middle_one = inputs + jnp.dot(attn_low, g_o, preferred_element_type=jnp.float32)
    normed_two, pull_two = jax.vjp(normalize, middle_one, pieces[2], pieces[3])
    h_second = normed_two.astype(jnp.bfloat16)
    cross_q = (
        jnp.dot(h_second, g_cq, preferred_element_type=jnp.float32)
        .astype(jnp.bfloat16)
        .reshape(row_count, HEADS, HEAD)
    )
    source_local = jnp.dot(encoded, g_ckv, preferred_element_type=jnp.float32).astype(jnp.bfloat16)
    source_all = lax.all_gather(source_local, "blk", axis=0, tiled=True)
    cross_k = source_all[:, :D].reshape(-1, HEADS, HEAD)
    cross_v = source_all[:, D:].reshape(-1, HEADS, HEAD)
    cross_raw = (
        jnp.einsum("qhd,khd->hqk", cross_q, cross_k, preferred_element_type=jnp.float32) * scaling
    )
    cross_prob = jax.nn.softmax(cross_raw, axis=-1)
    cross_low = cross_prob.astype(jnp.bfloat16)
    cross_out = (
        jnp.einsum("hqk,khd->qhd", cross_low, cross_v, preferred_element_type=jnp.float32)
        .reshape(row_count, D)
        .astype(jnp.bfloat16)
    )
    middle_two = middle_one + jnp.dot(cross_out, g_co, preferred_element_type=jnp.float32)
    normed_three, pull_three = jax.vjp(normalize, middle_two, pieces[4], pieces[5])
    h_third = normed_three.astype(jnp.bfloat16)
    hidden_pre = jnp.dot(h_third, g_in, preferred_element_type=jnp.float32)
    activated, pull_gelu = jax.vjp(
        lambda values_in: jax.nn.gelu(values_in, approximate=True), hidden_pre
    )
    act_low = activated.astype(jnp.bfloat16)
    result = middle_two + jnp.dot(act_low, g_out, preferred_element_type=jnp.float32)
    mixed_out = result.astype(jnp.bfloat16)
    back_weights = (
        lax.all_gather(w_qkv, ("leaf", "blk"), axis=0, tiled=True),
        lax.all_gather(w_o, ("leaf", "blk"), axis=0, tiled=True),
        lax.all_gather(w_cq, ("leaf", "blk"), axis=0, tiled=True),
        lax.all_gather(w_ckv, ("leaf", "blk"), axis=0, tiled=True),
        lax.all_gather(w_co, ("leaf", "blk"), axis=0, tiled=True),
        lax.all_gather(w_in, ("leaf", "blk"), axis=0, tiled=True),
        lax.all_gather(w_out, ("leaf", "blk"), axis=0, tiled=True),
        lax.all_gather(mod_table, ("leaf", "blk"), axis=1, tiled=True),
    )
    b_qkv, b_o, b_cq, b_ckv, b_co, b_in, b_out = back_weights[:7]
    d_act = jnp.dot(cotangent, b_out.T, preferred_element_type=jnp.float32)
    d_hidden = pull_gelu(d_act)[0].astype(jnp.bfloat16)
    grad_out_w = jnp.dot(act_low.T, cotangent, preferred_element_type=jnp.float32)
    grad_in_w = jnp.dot(h_third.T, d_hidden, preferred_element_type=jnp.float32)
    d_h_third = jnp.dot(d_hidden, b_in.T, preferred_element_type=jnp.float32)
    d_middle_part, d_shift_three, d_scale_three = pull_three(d_h_third)
    d_middle_two = cotangent.astype(jnp.float32) + d_middle_part
    d_branch_two = d_middle_two.astype(jnp.bfloat16)
    grad_co_w = jnp.dot(cross_out.T, d_branch_two, preferred_element_type=jnp.float32)
    d_cross_out = (
        jnp.dot(d_branch_two, b_co.T, preferred_element_type=jnp.float32)
        .astype(jnp.bfloat16)
        .reshape(row_count, HEADS, HEAD)
    )
    d_cross_prob = jnp.einsum(
        "qhd,khd->hqk", d_cross_out, cross_v, preferred_element_type=jnp.float32
    )
    d_cross_raw = (
        cross_prob * (d_cross_prob - jnp.sum(cross_prob * d_cross_prob, axis=-1, keepdims=True))
    ).astype(jnp.bfloat16)
    d_cross_q = (
        (
            jnp.einsum("hqk,khd->qhd", d_cross_raw, cross_k, preferred_element_type=jnp.float32)
            * scaling
        )
        .reshape(row_count, D)
        .astype(jnp.bfloat16)
    )
    d_cross_k = (
        jnp.einsum("hqk,qhd->khd", d_cross_raw, cross_q, preferred_element_type=jnp.float32)
        * scaling
    )
    d_cross_v = jnp.einsum(
        "hqk,qhd->khd", cross_low, d_cross_out, preferred_element_type=jnp.float32
    )
    source_terms = jnp.concatenate((d_cross_k.reshape(-1, D), d_cross_v.reshape(-1, D)), axis=1)
    d_source = lax.psum_scatter(
        source_terms.astype(jnp.bfloat16), "blk", scatter_dimension=0, tiled=True
    )
    grad_ckv_w = jnp.dot(encoded.T, d_source, preferred_element_type=jnp.float32)
    d_encoded = jnp.dot(d_source, b_ckv.T, preferred_element_type=jnp.float32)
    grad_cq_w = jnp.dot(h_second.T, d_cross_q, preferred_element_type=jnp.float32)
    d_h_second = jnp.dot(d_cross_q, b_cq.T, preferred_element_type=jnp.float32)
    d_middle_part, d_shift_two, d_scale_two = pull_two(d_h_second)
    d_middle_one = d_middle_two + d_middle_part
    d_branch_one = d_middle_one.astype(jnp.bfloat16)
    grad_o_w = jnp.dot(attn_low.T, d_branch_one, preferred_element_type=jnp.float32)
    d_attn = (
        jnp.dot(d_branch_one, b_o.T, preferred_element_type=jnp.float32)
        .astype(jnp.bfloat16)
        .reshape(row_count, HEADS, HEAD)
    )
    keys_back, values_back = (
        lax.all_gather(projected[:, D : 2 * D], "blk", axis=0, tiled=True),
        lax.all_gather(projected[:, 2 * D :], "blk", axis=0, tiled=True),
    )
    d_queries, key_terms = tree_backward_attention(
        queries, keys_back, values_back, reach_rows, first_block, log_total, d_attn
    )
    d_key_value = lax.psum_scatter(
        key_terms.astype(jnp.bfloat16), "blk", scatter_dimension=0, tiled=True
    ).astype(jnp.float32)
    d_projected = jnp.concatenate((d_queries.reshape(row_count, D), d_key_value), axis=1).astype(
        jnp.bfloat16
    )
    grad_qkv_w = jnp.dot(h_first.T, d_projected, preferred_element_type=jnp.float32)
    d_h_first = jnp.dot(d_projected, b_qkv.T, preferred_element_type=jnp.float32)
    d_input_part, d_shift_one, d_scale_one = pull_one(d_h_first)
    d_tokens = d_middle_one + d_input_part
    d_modulate = jnp.concatenate(
        (d_shift_one, d_scale_one, d_shift_two, d_scale_two, d_shift_three, d_scale_three)
    )
    grad_table_w = select[:, None] * d_modulate[None, :]
    gradients = (
        lax.psum_scatter(grad_qkv_w, ("leaf", "blk"), scatter_dimension=0, tiled=True),
        lax.psum_scatter(grad_o_w, ("leaf", "blk"), scatter_dimension=0, tiled=True),
        lax.psum_scatter(grad_cq_w, ("leaf", "blk"), scatter_dimension=0, tiled=True),
        lax.psum_scatter(grad_ckv_w, ("leaf", "blk"), scatter_dimension=0, tiled=True),
        lax.psum_scatter(grad_co_w, ("leaf", "blk"), scatter_dimension=0, tiled=True),
        lax.psum_scatter(grad_in_w, ("leaf", "blk"), scatter_dimension=0, tiled=True),
        lax.psum_scatter(grad_out_w, ("leaf", "blk"), scatter_dimension=0, tiled=True),
        lax.psum_scatter(grad_table_w, ("leaf", "blk"), scatter_dimension=1, tiled=True),
    )
    return (
        mixed_out,
        d_tokens,
        d_encoded,
        gradients[0],
        gradients[1],
        gradients[2],
        gradients[3],
        gradients[4],
        gradients[5],
        gradients[6],
        gradients[7],
    )


MESH = pl.DeviceIdType.MESH
BF = jnp.bfloat16
F32 = jnp.float32


class Place:
    def __init__(self, levels):
        leaf = lax.axis_index("leaf")
        blk = lax.axis_index("blk")
        self.levels = levels
        self.leaf = leaf
        self.blk = blk
        self.z = leaf // 2
        self.core = leaf % 2
        self.near = blk + 1 - 2 * (blk % 2)
        self.far = (blk + 2) % 4
        self.first = self.core * self.near + (1 - self.core) * self.far
        self.second = self.core * self.far + (1 - self.core) * self.near
        self.opposite = 3 - blk
        self.sibling = self.z * 2 + 1 - self.core
        self.has_up = self.z < levels - 1
        self.has_down = self.z > 0

    def greet(self):
        barrier = pltpu.get_barrier_semaphore()

        def hello(leaf, blk):
            pl.semaphore_signal(barrier, inc=1, device_id=(leaf, blk), device_id_type=MESH)

        hello(self.sibling, self.blk)
        hello(self.leaf, self.near)
        hello(self.leaf, self.far)
        hello(self.leaf, self.opposite)
        pl.when(self.has_up)(lambda: hello(self.leaf + 2, self.blk))
        pl.when(self.has_down)(lambda: hello(self.leaf - 2, self.blk))
        ends = self.has_up.astype(jnp.int32) + self.has_down.astype(jnp.int32)
        pl.semaphore_wait(barrier, 4 + ends)


def remote(src, dst, send, recv, leaf, blk):
    return pltpu.make_async_remote_copy(
        src_ref=src, dst_ref=dst, send_sem=send, recv_sem=recv,
        device_id=(leaf, blk), device_id_type=MESH,
    )


def under(cond, action):
    if cond is None:
        action()
    else:
        pl.when(cond)(action)


def both(one, two):
    if one is None:
        return two
    if two is None:
        return one
    return jnp.logical_and(one, two)


def rows_of(start, count):
    return pl.ds(pl.multiple_of(start * count, count), count)


class Gather:
    def __init__(self, place, own, full, rows, columns, send_sem, recv_sem):
        self.place, self.own, self.full, self.rows, self.columns = place, own, full, rows, columns
        self.send_sem, self.recv_sem = send_sem, recv_sem
        self.sent = []
        self.count = 0

    def view(self, leaf, blk):
        return self.full.at[rows_of(leaf * 4 + blk, self.rows), self.columns]

    def push(self, leaf, blk, targets, cond, own=False):
        for to_leaf, to_blk, needs in targets:
            number = self.count
            self.count += 1

            def build(number=number, to_leaf=to_leaf, to_blk=to_blk):
                there = self.view(leaf, blk)
                return remote(
                    self.own if own else there, there, self.send_sem.at[number],
                    self.recv_sem.at[leaf * 4 + blk], to_leaf, to_blk,
                )

            ok = both(cond, needs)
            under(ok, lambda: build().start())
            self.sent.append((ok, build))

    def arrive(self, leaf, blk, cond=None):
        p = self.place

        def wait():
            there = self.view(leaf, blk)
            remote(there, there, self.send_sem.at[0], self.recv_sem.at[leaf * 4 + blk], p.leaf, p.second).wait_recv()

        under(cond, wait)

    def to(self, *names):
        p = self.place
        table = {
            "sibling": (p.sibling, p.blk, None),
            "first": (p.leaf, p.first, None),
            "second": (p.leaf, p.second, None),
            "up": (p.leaf + 2, p.blk, p.has_up),
            "down": (p.leaf - 2, p.blk, p.has_down),
        }
        return [table[name] for name in names]

    def steps(self):
        p = self.place
        self.push(p.leaf, p.blk, self.to("first", "up", "down", "second", "sibling"), None, own=True)
        yield
        self.arrive(p.leaf, p.first)
        self.push(p.leaf, p.first, self.to("up", "down", "second", "sibling"), None)
        yield
        for k in range(1, p.levels):
            below, above = p.leaf - 2 * k, p.leaf + 2 * k
            has_below, has_above = p.z >= k, p.z + k < p.levels
            for blk in (p.blk, p.first):
                self.arrive(below, blk, has_below)
                self.push(below, blk, self.to("up", "second", "sibling"), has_below)
                self.arrive(above, blk, has_above)
                self.push(above, blk, self.to("down", "second", "sibling"), has_above)
            yield
        for k in range(p.levels):
            for leaf, cond in ((p.leaf - 2 * k, p.z >= k), (p.leaf + 2 * k, p.z + k < p.levels)):
                if k == 0 and leaf is not None:
                    cond = None
                for blk in (p.second, p.opposite):
                    self.arrive(leaf, blk, cond)
                    self.push(leaf, blk, self.to("sibling"), cond)
                if k == 0:
                    break
            yield
        for level in range(p.levels):
            for blk in range(4):
                self.arrive(2 * level + 1 - p.core, blk)
        yield

    def finish(self):
        for ok, build in self.sent:
            under(ok, lambda build=build: build().wait_send())

    @staticmethod
    def sends(levels):
        return 5 + 4 + (levels - 1) * 12 + 2 + (levels - 1) * 4


class Share:
    def __init__(self, place, own, full, rows, send_sem, recv_sem):
        self.place, self.own, self.full, self.rows = place, own, full, rows
        self.send_sem, self.recv_sem = send_sem, recv_sem
        self.half = rows // 2

    def view(self, blk, half):
        return self.full.at[pl.ds(pl.multiple_of(blk * self.rows + half * self.half, self.half), self.half), :]

    def build(self, blk, half, to_blk, number, own=False):
        there = self.view(blk, half)
        src = self.own.at[pl.ds(half * self.half, self.half), :] if own else there
        return remote(src, there, self.send_sem.at[number], self.recv_sem.at[blk * 2 + half], self.place.leaf, to_blk)

    def steps(self):
        p = self.place
        self.copies = [
            self.build(p.blk, 0, p.near, 0, True),
            self.build(p.blk, 1, p.far, 1, True),
            self.build(p.blk, 1, p.near, 2, True),
            self.build(p.blk, 0, p.far, 3, True),
        ]
        for copy in self.copies:
            copy.start()
        yield
        for blk, half, to_blk, number in ((p.near, 0, p.far, 4), (p.far, 1, p.near, 5)):
            copy = self.build(blk, half, to_blk, number)
            copy.wait_recv()
            copy.start()
            self.copies.append(copy)
        yield
        self.build(p.near, 1, p.near, 0).wait_recv()
        self.build(p.far, 0, p.near, 0).wait_recv()
        yield
        self.build(p.opposite, 0, p.near, 0).wait_recv()
        self.build(p.opposite, 1, p.near, 0).wait_recv()
        yield

    def finish(self):
        for copy in self.copies:
            copy.wait_send()


class Spread:
    def __init__(self, place, own, full, rows, send_sem, recv_sem):
        self.place, self.own, self.full, self.rows = place, own, full, rows
        self.send_sem, self.recv_sem = send_sem, recv_sem

    def build(self, src, blk, to_blk, number):
        there = self.full.at[rows_of(blk, self.rows), :]
        return remote(there if src is None else src, there, self.send_sem.at[number], self.recv_sem.at[blk], self.place.leaf, to_blk)

    def start(self):
        p = self.place
        self.copies = [self.build(self.own, p.blk, to, n) for n, to in enumerate((p.near, p.far, p.opposite))]
        for copy in self.copies:
            copy.start()

    def arrive(self):
        p = self.place
        for blk in (p.near, p.far, p.opposite):
            self.build(None, blk, p.near, 0).wait_recv()

    def finish(self):
        for copy in self.copies:
            copy.wait_send()


class Reduce:
    def __init__(self, place, total, rows, columns, out, boxes, send_sem, recv_sem):
        self.place, self.total, self.rows, self.columns, self.out = place, total, rows, columns, out
        self.from_sibling, self.from_second, self.from_below, self.from_above, self.from_first = boxes
        self.send_sem, self.recv_sem = send_sem, recv_sem
        self.sent = []

    @staticmethod
    def slots(levels):
        return 7 * levels + 1

    @staticmethod
    def boxes(levels, rows, width, kind):
        return [
            pltpu.VMEM((levels * 4 * rows, width), kind),
            pltpu.VMEM((levels * 2 * rows, width), kind),
            pltpu.VMEM((levels * 2 * rows, width), kind),
            pltpu.VMEM((levels * 2 * rows, width), kind),
            pltpu.VMEM((rows, width), kind),
        ]

    def part(self, leaf, blk, count=1):
        return self.total.at[pl.ds(pl.multiple_of((leaf * 4 + blk) * self.rows, self.rows), self.rows * count), self.columns]

    def copy(self, src, box, position, count, number, leaf, blk):
        there = box.at[pl.ds(pl.multiple_of(position * self.rows, self.rows), self.rows * count), :]
        return remote(there if src is None else src, there, self.send_sem.at[number], self.recv_sem.at[number], leaf, blk)

    def send(self, cond, *parts):
        under(cond, lambda: self.copy(*parts).start())
        self.sent.append((cond, parts))

    def arrived(self, box, position, count, number):
        self.copy(None, box, position, count, number, self.place.leaf, self.place.first).wait_recv()

    def add(self, leaf, blk, box, position, count=1):
        unit = 16 if self.rows % 16 == 0 else self.rows
        into = (leaf * 4 + blk) * self.rows
        source = position * self.rows

        def one(step, carry):
            here = pl.ds(pl.multiple_of(into + step * unit, unit), unit)
            there = pl.ds(pl.multiple_of(source + step * unit, unit), unit)
            value = self.total[here, self.columns].astype(F32) + box[there, :].astype(F32)
            self.total[here, self.columns] = value.astype(self.total.dtype)
            return carry

        lax.fori_loop(0, count * self.rows // unit, one, 0)

    def steps(self):
        p = self.place
        levels = p.levels
        for level in range(levels):
            self.send(None, self.part(2 * level + 1 - p.core, 0, 4), self.from_sibling, 4 * level, 4, level, p.sibling, p.blk)
        yield
        for level in range(levels):
            self.arrived(self.from_sibling, 4 * level, 4, level)
            leaf = 2 * level + p.core
            self.add(leaf, 0, self.from_sibling, 4 * level, 4)
            for which, blk in enumerate((p.second, p.opposite)):
                slot = 2 * level + which
                self.send(None, self.part(leaf, blk), self.from_second, slot, 1, levels + slot, p.leaf, p.second)
        yield
        for level in range(levels):
            leaf = 2 * level + p.core
            for which, blk in enumerate((p.blk, p.first)):
                slot = 2 * level + which
                self.arrived(self.from_second, slot, 1, levels + slot)
                self.add(leaf, blk, self.from_second, slot)
        yield
        for k in range(levels - 1, -1, -1):
            for which, blk in enumerate((p.blk, p.first)):
                up, down = 2 * (p.z + k) + which, 2 * (p.z - k) + which

                def climb(up=up, blk=blk):
                    def more():
                        self.arrived(self.from_below, up, 1, 3 * levels + up)
                        self.add(p.leaf + 2 * k, blk, self.from_below, up)

                    pl.when(p.has_down)(more)

                def fall(down=down, blk=blk):
                    def more():
                        self.arrived(self.from_above, down, 1, 5 * levels + down)
                        self.add(p.leaf - 2 * k, blk, self.from_above, down)

                    pl.when(p.has_up)(more)

                if k == 0:
                    climb()
                    fall()
                else:
                    can_up, can_down = p.z + k < levels, p.z >= k
                    under(can_up, climb)
                    self.send(can_up, self.part(p.leaf + 2 * k, blk), self.from_below, up, 1, 3 * levels + up, p.leaf + 2, p.blk)
                    under(can_down, fall)
                    self.send(can_down, self.part(p.leaf - 2 * k, blk), self.from_above, down, 1, 5 * levels + down, p.leaf - 2, p.blk)
            yield
        self.send(None, self.part(p.leaf, p.first), self.from_first, 0, 1, 7 * levels, p.leaf, p.first)
        yield
        self.arrived(self.from_first, 0, 1, 7 * levels)
        unit = 16 if self.rows % 16 == 0 else self.rows
        for step in range(self.rows // unit):
            here = pl.ds(pl.multiple_of((p.leaf * 4 + p.blk) * self.rows + step * unit, unit), unit)
            there = pl.ds(step * unit, unit)
            self.out(there, self.total[here, self.columns].astype(F32) + self.from_first[there, :].astype(F32))
        yield

    def finish(self):
        for cond, parts in self.sent:
            under(cond, lambda parts=parts: self.copy(*parts).wait_send())


def run_all(sequences):
    live = [item.steps() for item in sequences]
    while live:
        live = [item for item in live if next(item, "end") != "end"]


class GatherPair:
    def __init__(self, place, own, full, send_sem, recv_sem):
        self.place, self.own, self.full = place, own, full
        self.rows, self.width = own.shape[0], full.shape[1]
        self.send_sem, self.recv_sem = send_sem, recv_sem
        self.sent = []
        self.count = 0

    def start(self, cond, make):
        under(cond, lambda: make().start())
        self.sent.append((cond, make))

    def piece(self, src_blk, to_blk, number, own):
        p = self.place
        there = self.full.at[rows_of(p.leaf * 4 + src_blk, self.rows), :]
        src = self.own.at[:, pl.ds(pl.multiple_of(to_blk * self.width, self.width), self.width)] if own else there
        return remote(src, there, self.send_sem.at[number], self.recv_sem.at[src_blk], p.leaf, to_blk)

    def block(self, leaf, number, to_leaf):
        there = self.full.at[rows_of(leaf, 4 * self.rows), :]
        return remote(there, there, self.send_sem.at[number], self.recv_sem.at[4 + leaf], to_leaf, self.place.blk)

    def push(self, leaf, cond, names):
        p = self.place
        table = {"sibling": (p.sibling, None), "up": (p.leaf + 2, p.has_up), "down": (p.leaf - 2, p.has_down)}
        for name in names:
            to_leaf, needs = table[name]
            number = 3 + self.count
            self.count += 1
            self.start(both(cond, needs), lambda number=number, to_leaf=to_leaf: self.block(leaf, number, to_leaf))

    def wait(self, leaf, cond):
        under(cond, lambda: self.block(leaf, 0, self.place.sibling).wait_recv())

    def local(self, sem):
        p = self.place
        mine = self.own.at[:, pl.ds(pl.multiple_of(p.blk * self.width, self.width), self.width)]
        return pltpu.make_async_copy(mine, self.full.at[rows_of(p.leaf * 4 + p.blk, self.rows), :], sem)

    def steps(self):
        p = self.place
        for number, to_blk in enumerate((p.near, p.far, p.opposite)):
            self.start(None, lambda to_blk=to_blk, number=number: self.piece(p.blk, to_blk, number, True))
        yield
        for blk in (p.near, p.far, p.opposite):
            self.piece(blk, p.near, 0, False).wait_recv()
        self.push(p.leaf, None, ("up", "down", "sibling"))
        yield
        for k in range(1, p.levels):
            below, above = p.leaf - 2 * k, p.leaf + 2 * k
            has_below, has_above = p.z >= k, p.z + k < p.levels
            self.wait(below, has_below)
            self.push(below, has_below, ("up", "sibling"))
            self.wait(above, has_above)
            self.push(above, has_above, ("down", "sibling"))
            yield
        for level in range(p.levels):
            self.wait(2 * level + 1 - p.core, None)
        yield

    def finish(self):
        for cond, make in self.sent:
            under(cond, lambda make=make: make().wait_send())

    @staticmethod
    def sends(levels):
        return 6 + 4 * (levels - 1)


class ReducePair:
    def __init__(self, place, total, out, boxes, send_sem, recv_sem):
        self.place, self.total, self.out = place, total, out
        self.rows = total.shape[0] // (place.levels * 8)
        self.from_sibling, self.from_below, self.from_above, self.from_pair = boxes
        self.send_sem, self.recv_sem = send_sem, recv_sem
        self.sent = []

    @staticmethod
    def slots(levels):
        return 3 * levels + 4

    @staticmethod
    def boxes(levels, rows, width, kind):
        return [pltpu.VMEM((levels * 4 * rows, width), kind) for n in range(3)] + [pltpu.VMEM((4 * rows, width), kind)]

    def send(self, cond, src, box, slot, rows, number, leaf, blk):
        def make():
            there = box.at[rows_of(slot, rows), :]
            return remote(there if src is None else src, there, self.send_sem.at[number], self.recv_sem.at[number], leaf, blk)

        under(cond, lambda: make().start())
        self.sent.append((cond, make))

    def arrived(self, box, slot, rows, number):
        there = box.at[rows_of(slot, rows), :]
        p = self.place
        remote(there, there, self.send_sem.at[0], self.recv_sem.at[number], p.sibling, p.blk).wait_recv()

    def part(self, leaf):
        return self.total.at[rows_of(leaf, 4 * self.rows), :]

    def add(self, leaf, box, slot):
        here, there = rows_of(leaf, 4 * self.rows), rows_of(slot, 4 * self.rows)
        value = self.total[here, :].astype(F32) + box[there, :].astype(F32)
        self.total[here, :] = value.astype(self.total.dtype)

    def steps(self):
        p = self.place
        levels, rows = p.levels, 4 * self.rows
        for level in range(levels):
            self.send(None, self.part(2 * level + 1 - p.core), self.from_sibling, level, rows, level, p.sibling, p.blk)
        yield
        for level in range(levels):
            self.arrived(self.from_sibling, level, rows, level)
            self.add(2 * level + p.core, self.from_sibling, level)
        yield
        for k in range(levels - 1, -1, -1):
            up, down = p.z + k, p.z - k

            def climb():
                def more():
                    self.arrived(self.from_below, up, rows, levels + up)
                    self.add(p.leaf + 2 * k, self.from_below, up)

                pl.when(p.has_down)(more)

            def fall():
                def more():
                    self.arrived(self.from_above, down, rows, 2 * levels + down)
                    self.add(p.leaf - 2 * k, self.from_above, down)

                pl.when(p.has_up)(more)

            if k == 0:
                climb()
                fall()
            else:
                under(up < levels, climb)
                self.send(up < levels, self.part(p.leaf + 2 * k), self.from_below, up, rows, levels + up, p.leaf + 2, p.blk)
                under(down >= 0, fall)
                self.send(down >= 0, self.part(p.leaf - 2 * k), self.from_above, down, rows, 2 * levels + down, p.leaf - 2, p.blk)
            yield
        for to_blk in (p.near, p.far, p.opposite):
            src = self.total.at[rows_of(p.leaf * 4 + to_blk, self.rows), :]
            self.pair_send(src, to_blk)
        yield
        self.store(p.blk, self.total[rows_of(p.leaf * 4 + p.blk, self.rows), :])
        for blk in (p.near, p.far, p.opposite):
            there = self.from_pair.at[rows_of(blk, self.rows), :]
            remote(there, there, self.send_sem.at[0], self.recv_sem.at[3 * levels + blk], p.leaf, p.near).wait_recv()
            self.store(blk, self.from_pair[rows_of(blk, self.rows), :])
        yield

    def pair_send(self, src, to_blk):
        p = self.place

        def make():
            there = self.from_pair.at[rows_of(p.blk, self.rows), :]
            return remote(src, there, self.send_sem.at[3 * p.levels + to_blk], self.recv_sem.at[3 * p.levels + p.blk], p.leaf, to_blk)

        make().start()
        self.sent.append((None, make))

    def store(self, blk, value):
        for third in range(3):
            lanes = pl.ds(pl.multiple_of(third * D + blk * 128, 128), 128)
            self.out[:, lanes] = value[:, third * 128:third * 128 + 128].astype(F32)

    def finish(self):
        for cond, make in self.sent:
            under(cond, lambda make=make: make().wait_send())


class Settle:
    def __init__(self, place, part, out, box, send_sem, recv_sem):
        self.place, self.part, self.out, self.box = place, part, out, box
        self.send_sem, self.recv_sem = send_sem, recv_sem
        self.rows = out.shape[0]

    def build(self, src_blk, to_blk):
        p = self.place
        return remote(self.part.at[rows_of(to_blk, self.rows), :], self.box.at[rows_of(src_blk, self.rows), :],
                      self.send_sem.at[to_blk], self.recv_sem.at[src_blk], p.leaf, to_blk)

    def steps(self):
        p = self.place
        self.copies = [self.build(p.blk, to) for to in (p.near, p.far, p.opposite)]
        for copy in self.copies:
            copy.start()
        yield
        total = self.part[rows_of(p.blk, self.rows), :]
        for blk in (p.near, p.far, p.opposite):
            self.build(blk, p.near).wait_recv()
            total = total + self.box[rows_of(blk, self.rows), :]
        self.out[...] = total
        yield

    def finish(self):
        for copy in self.copies:
            copy.wait_send()


SPAN = 256
TINY = 1e-05


def dot(left, right):
    return lax.dot_general(left, right, (((1,), (0,)), ((), ())), preferred_element_type=F32)


def dot_nt(left, right):
    return lax.dot_general(left, right, (((1,), (1,)), ((), ())), preferred_element_type=F32)


def dot_tn(left, right):
    return lax.dot_general(left, right, (((0,), (0,)), ((), ())), preferred_element_type=F32)


def iota(shape, axis):
    return lax.broadcasted_iota(jnp.int32, shape, axis)


def span(start, count=SPAN):
    return pl.ds(pl.multiple_of(start * count, count), count)


def loop(count, body):
    def step(index, carry):
        body(index)
        return carry

    lax.fori_loop(0, count, step, 0)


def unit_rows(values):
    centred = values - jnp.mean(values, axis=-1, keepdims=True)
    root = lax.rsqrt(jnp.mean(centred * centred, axis=-1, keepdims=True) + TINY)
    return centred * root, root


def norm_back(grad, unit, root, scale):
    inner = grad * (1.0 + scale)
    return (
        inner
        - jnp.mean(inner, axis=-1, keepdims=True)
        - unit * jnp.mean(inner * unit, axis=-1, keepdims=True)
    ) * root


def spread_pattern(wide, group):
    column = iota((128, group), 1)
    turn = jnp.zeros((128, group), jnp.int32)
    for step in range(1, group // wide):
        turn = turn + (column >= step * wide).astype(jnp.int32)
    return (column - turn * wide == iota((128, group), 0)).astype(F32)


def shard_of_column(count, wide, group):
    column = iota((count, group), 1)
    turn = jnp.zeros((count, group), jnp.int32)
    for step in range(1, group // wide):
        turn = turn + (column >= step * wide).astype(jnp.int32)
    return turn


def read_modulation(aux, timestep, mod, wide):
    count = aux.shape[0] // 64
    row = iota((count, aux.shape[0]), 0)
    column = iota((count, aux.shape[0]), 1)
    chosen = (column == row * 64 + timestep).astype(BF)
    picked = dot(chosen, aux[...])
    group = wide * 4
    laid = dot(picked.astype(BF), spread_pattern(wide, group).astype(BF))
    offset = iota((count, group), 0) - shard_of_column(count, wide, group)
    for part in range(count // 4):
        mod[0:1, part * group:(part + 1) * group] = jnp.sum(
            jnp.where(offset == 4 * part, laid, 0.0), axis=0, keepdims=True
        )


def table_payload(sums, leaf, wide, count):
    group = wide * 4
    offset = iota((count, group), 0) - shard_of_column(count, wide, group)
    held = jnp.zeros((count, group), F32)
    for part in range(count // 4):
        held = held + jnp.where(offset == 4 * part, sums[0:1, part * group:(part + 1) * group], 0.0)
    cut = lax.dot_general(held, spread_pattern(wide, group), (((1,), (1,)), ((), ())),
                          preferred_element_type=F32, precision=lax.Precision.HIGHEST)
    row = iota((count * 8, count), 0)
    chosen = (row == iota((count * 8, count), 1) * 8 + leaf).astype(F32)
    return lax.dot_general(chosen, cut, (((1,), (0,)), ((), ())),
                           preferred_element_type=F32, precision=lax.Precision.HIGHEST)


def block_bias(parents, bias, blocks):
    row, column = iota((128, 128), 0), iota((128, 128), 1)
    reach = (row == column).astype(F32)
    for block in range(blocks):
        reach = jnp.maximum(reach, ((column == block) & (row == parents[0, block])).astype(F32))
    for step in range((blocks - 1).bit_length()):
        low_reach = reach.astype(BF)
        reach = jnp.minimum(dot(low_reach, low_reach), 1.0)
    held = (reach[:blocks, :] - 1.0) * 1e30
    for block in range(blocks):
        bias[:, block * BLOCK:(block + 1) * BLOCK] = jnp.broadcast_to(held[:, block:block + 1], (blocks, BLOCK))


class Layer:
    def __init__(self, place, refs):
        self.place = place
        self.__dict__.update(refs)

    def project(self, chunk):
        rows = span(chunk)
        unit, root = unit_rows(self.tokens_all[rows, :].astype(F32))
        first = (unit * (1.0 + self.mod[0:1, D:2 * D]) + self.mod[0:1, 0:D]).astype(BF)
        self.h1[rows, :] = first
        made = dot(first, self.w_pair[...])
        lane = iota((SPAN, 128), 1)
        query = made[:, 0:128].astype(BF).astype(F32) * HEAD ** (-0.5)
        self.q_masked[0, rows, :] = jnp.where(lane < HEAD, query, 0.0).astype(BF)
        self.q_masked[1, rows, :] = jnp.where(lane >= HEAD, query, 0.0).astype(BF)
        key = made[:, 128:256]
        value = made[:, 256:384]
        self.key[rows, :] = key.astype(BF)
        self.value[rows, :] = value.astype(BF)
        self.key_t[:, rows] = key.T.astype(BF)
        value_t = value.T.astype(BF)
        ones = jnp.ones((16, SPAN), BF)
        self.value_t[0, 0:HEAD, rows] = value_t[:HEAD]
        self.value_t[1, 0:HEAD, rows] = value_t[HEAD:]
        self.value_t[0, HEAD:HEAD + 16, rows] = ones
        self.value_t[1, HEAD:HEAD + 16, rows] = ones

    def attend(self, tile):
        queries = span(tile)
        base = tile * (tile + 1) // 2
        self.top[...] = jnp.full_like(self.top, -3e30)

        def score(j, diagonal):
            keys = span(j)
            for head in range(2):
                raw = dot_nt(self.key[keys, :], self.q_masked[head, queries, :])
                upper = raw[:BLOCK] + self.bias[pl.ds(2 * j, 1), queries]
                lower = raw[BLOCK:] + self.bias[pl.ds(2 * j + 1, 1), queries]
                kept = jnp.concatenate((upper, lower), axis=0)
                if diagonal:
                    kept = kept + self.corner[...]
                self.scores[head, keys, :] = kept
                self.top[head] = jnp.maximum(self.top[head], jnp.max(kept.reshape(SPAN // 8, 8, SPAN), axis=0))

        loop(tile, lambda j: score(j, False))
        score(tile, True)
        top = [jnp.max(self.top[head], axis=0, keepdims=True) for head in range(2)]
        self.mix[...] = jnp.zeros_like(self.mix)

        def weigh(j):
            keys = span(j)
            for head in range(2):
                weight = jnp.exp(self.scores[head, keys, :] - top[head]).astype(BF)
                self.weights[base + j, head] = weight
                self.mix[head] += dot(self.value_t[head, :, keys], weight)

        loop(tile + 1, weigh)
        halves = []
        for head in range(2):
            inverse = 1.0 / self.mix[head, HEAD:HEAD + 8, :]
            self.inverse[head, :, queries] = inverse
            halves.append(self.mix[head, :HEAD, :] * inverse[0:1])
        attended_t = jnp.concatenate(halves, axis=0)
        self.attended_t[:, queries] = attended_t
        self.attended[queries, :] = attended_t.T.astype(BF)

    def cross_keys(self):
        made = dot(self.source_all[...], self.w_ckv).astype(BF)
        lane = iota((2 * ENC, 128), 1)
        row = iota((2 * ENC, 128), 0)
        own = (lane < HEAD) == (row < ENC)
        for pair in range(4):
            for box, start in ((self.cross_k, 0), (self.cross_v, D)):
                part = made[:, start + 128 * pair:start + 128 * pair + 128].astype(F32)
                box[pair] = jnp.where(own, jnp.concatenate((part, part), axis=0), 0.0).astype(BF)

    def middle(self, chunk):
        rows = span(chunk)
        own = span(self.place.blk * (self.tokens_rows // SPAN) + chunk)
        y1 = self.tokens_all[own, :].astype(F32) + dot(self.gathered[rows, :], self.w_o)
        self.y1[rows, :] = y1
        unit, root = unit_rows(y1)
        h2 = (unit * (1.0 + self.mod[0:1, 3 * D:4 * D]) + self.mod[0:1, 2 * D:3 * D]).astype(BF)
        self.h2[rows, :] = h2
        query = (dot(h2, self.w_cq).astype(BF).astype(F32) * HEAD ** (-0.5)).astype(BF)
        self.cross_q[rows, :] = query
        lane = iota((SPAN, 128), 1)
        same = ((iota((128, 128), 0) < ENC) == (iota((128, 128), 1) < ENC)).astype(BF)
        out = []
        for pair in range(4):
            raw = dot_nt(query[:, 128 * pair:128 * pair + 128], self.cross_k[pair])
            left = jnp.max(jnp.where(lane < ENC, raw, -3e38), axis=-1, keepdims=True)
            right = jnp.max(jnp.where(lane >= ENC, raw, -3e38), axis=-1, keepdims=True)
            weight = jnp.exp(raw - jnp.where(lane < ENC, left, right))
            weight = weight / dot(weight.astype(BF), same)
            self.cross_p[pair, rows, :] = weight
            out.append(dot(weight.astype(BF), self.cross_v[pair]))
        cross = jnp.concatenate(out, axis=1).astype(BF)
        self.cross_out[rows, :] = cross
        y2 = y1 + dot(cross, self.w_co)
        self.y2[rows, :] = y2
        unit, root = unit_rows(y2)
        self.h3[rows, :] = (unit * (1.0 + self.mod[0:1, 5 * D:6 * D]) + self.mod[0:1, 4 * D:5 * D]).astype(BF)

    def hidden(self, chunk):
        units = span(chunk)
        u = dot(self.h3[...], self.w_in(units))
        dg = dot_nt(self.cotangent[...], self.w_out[units, :])
        square = u * u
        slope = 0.7978845608028654
        bend = jnp.tanh(u * (slope + slope * 0.044715 * square))
        half = 0.5 + 0.5 * bend
        self.act[:, units] = (u * half).astype(BF)
        turn = half + 0.5 * u * (1.0 - bend * bend) * (slope + 3.0 * slope * 0.044715 * square)
        self.d_hidden[:, units] = (dg * turn).astype(BF)
        self.grad_out(units, dot_tn(self.act[:, units], self.cotangent[...]).astype(BF))
        self.grad_in(units, dot_tn(self.h3[...], self.d_hidden[:, units]).astype(BF))

    def finish_forward(self, chunk):
        rows = span(chunk)
        self.mixed[rows, :] = (self.y2[rows, :] + dot(self.act[rows, :], self.w_out[...])).astype(BF)

    def sums(self, piece, shift, scale):
        self.mod_grad[0:1, 2 * piece * D:(2 * piece + 1) * D] += jnp.sum(shift, axis=0, keepdims=True)
        self.mod_grad[0:1, (2 * piece + 1) * D:(2 * piece + 2) * D] += jnp.sum(scale, axis=0, keepdims=True)

    def back_three(self, chunk):
        rows = span(chunk)
        dh3 = dot_nt(self.d_hidden[rows, :], self.w_in(slice(None)))
        unit, root = unit_rows(self.y2[rows, :])
        self.sums(2, dh3, dh3 * unit)
        dy2 = self.cotangent[rows, :].astype(F32) + norm_back(dh3, unit, root, self.mod[0:1, 5 * D:6 * D])
        self.dy[rows, :] = dy2
        self.db[rows, :] = dy2.astype(BF)

    def back_cross(self, chunk):
        rows = span(chunk)
        dca = dot_nt(self.db[rows, :], self.w_co).astype(BF)
        lane = iota((SPAN, 128), 1)
        row = iota((128, 128), 0)
        own = (row < ENC) == (iota((128, 128), 1) < HEAD)
        parts = []
        for pair in range(4):
            lanes = slice(128 * pair, 128 * pair + 128)
            weight = self.cross_p[pair, rows, :]
            dc = dot_nt(dca[:, lanes], self.cross_v[pair])
            both_ = weight * dc
            left = jnp.sum(jnp.where(lane < ENC, both_, 0.0), axis=-1, keepdims=True)
            right = jnp.sum(jnp.where(lane >= ENC, both_, 0.0), axis=-1, keepdims=True)
            ds = (weight * (dc - jnp.where(lane < ENC, left, right))).astype(BF)
            parts.append((dot(ds, self.cross_k[pair]) * HEAD ** (-0.5)).astype(BF))
            dk = jnp.where(own, dot_tn(ds, self.cross_q[rows, lanes]), 0.0)
            dv = jnp.where(own, dot_tn(weight.astype(BF), dca[:, lanes]), 0.0)
            self.d_cross[:, lanes] += dk[:ENC] + dk[ENC:]
            self.d_cross[:, 128 * pair + D:128 * pair + D + 128] += dv[:ENC] + dv[ENC:]
        dcq = jnp.concatenate(parts, axis=1)
        self.dcq[rows, :] = dcq
        dh2 = dot_nt(dcq, self.w_cq)
        unit, root = unit_rows(self.y1[rows, :])
        self.sums(1, dh2, dh2 * unit)
        dy1 = self.dy[rows, :] + norm_back(dh2, unit, root, self.mod[0:1, 3 * D:4 * D])
        self.dy[rows, :] = dy1
        low_dy1 = dy1.astype(BF)
        self.db1[rows, :] = low_dy1
        self.d_attn[rows, :] = dot_nt(low_dy1, self.w_o).astype(BF)

    def attend_back(self, tile):
        queries = span(tile)
        base = tile * (tile + 1) // 2
        d_att_t = self.d_att_all[queries, :].astype(F32).T
        scaled = [d_att_t[HEAD * h:HEAD * h + HEAD] * self.inverse[h, 0:1, queries] for h in range(2)]
        delta = [
            jnp.sum(scaled[h] * self.attended_t[HEAD * h:HEAD * h + HEAD, queries], axis=0, keepdims=True)
            for h in range(2)
        ]
        flat = jnp.concatenate(scaled, axis=0).T
        lane = iota((SPAN, 128), 1)
        self.d_masked[0] = jnp.where(lane < HEAD, flat, 0.0).astype(BF)
        self.d_masked[1] = jnp.where(lane >= HEAD, flat, 0.0).astype(BF)
        self.dq_t[...] = jnp.zeros_like(self.dq_t)

        def visit(j):
            keys = span(j)
            dk = dv = 0.0
            for head in range(2):
                dp = dot_nt(self.value[keys, :], self.d_masked[head])
                weight = self.weights[base + j, head]
                ds = (weight.astype(F32) * (dp - delta[head])).astype(BF)
                dk = dk + dot(ds, self.q_masked[head, queries, :])
                dv = dv + dot(weight, self.d_masked[head])
                self.dq_t[HEAD * head:HEAD * head + HEAD, :] += dot(self.key_t[HEAD * head:HEAD * head + HEAD, keys], ds)
            self.dk[keys, :] += dk
            self.dv[keys, :] += dv

        loop(tile + 1, visit)
        self.d_pair[queries, 0:128] = (self.dq_t[...] * HEAD ** (-0.5)).T.astype(BF)
        self.d_pair[queries, 128:256] = self.dk[queries, :].astype(BF)
        self.d_pair[queries, 256:384] = self.dv[queries, :].astype(BF)
        self.dh1_part[queries, :] = dot_nt(self.d_pair[queries, :], self.w_pair[...]).astype(BF)


ANY = pl.BlockSpec(memory_space=pl.ANY)
VMEM = pl.BlockSpec(memory_space=pltpu.VMEM)
SMEM = pl.BlockSpec(memory_space=pltpu.SMEM)
CUTS = ((0, 2560), (2560, FF))


def gather_kernel(levels, refs):
    (pair, pack, w_out, table, tokens, source, full_pair, full_pack, full_out, full_table, full_tokens, full_source,
     send, recv, pair_send, pair_recv, share_send, share_recv, spread_send, spread_recv, local) = refs
    place = Place(levels)
    rows = pack.shape[0]
    index = place.leaf * 4 + place.blk
    pairs = [
        (pack, full_pack.at[rows_of(index, rows), :]),
        (w_out, full_out.at[rows_of(index, w_out.shape[0]), :]),
        (table, full_table.at[rows_of(index, table.shape[0]), :]),
        (tokens, full_tokens.at[rows_of(place.blk, tokens.shape[0]), :]),
        (source, full_source.at[rows_of(place.blk, source.shape[0]), :]),
    ]
    weave = GatherPair(place, pair, full_pair, pair_send, pair_recv)
    mine = weave.local(local.at[5])
    mine.start()
    locals_ = [pltpu.make_async_copy(src, dst, local.at[n]) for n, (src, dst) in enumerate(pairs)]
    for copy in locals_:
        copy.start()
    place.greet()
    mine.wait()
    jobs = [Gather(place, table, full_table, table.shape[0], slice(None), send.at[0], recv.at[0])]
    for n, (start, width) in enumerate(CUTS):
        columns = pl.ds(start, width)
        jobs.append(Gather(place, pack.at[:, columns], full_pack, rows, columns, send.at[n + 1], recv.at[n + 1]))
    last = len(jobs)
    jobs.append(Gather(place, w_out, full_out, w_out.shape[0], slice(None), send.at[last], recv.at[last]))
    spread = Spread(place, source, full_source, source.shape[0], spread_send, spread_recv)
    spread.start()
    share = Share(place, tokens, full_tokens, tokens.shape[0], share_send, share_recv)
    run_all([weave, share] + jobs)
    spread.arrive()
    for job in jobs + [share, spread, weave]:
        job.finish()
    for copy in locals_:
        copy.wait()


def gather_all(levels, pair, pack, w_out, table, tokens, source):
    count = levels * 8
    shape = lambda rows, like: jax.ShapeDtypeStruct((rows, like.shape[1]), like.dtype)
    jobs = len(CUTS) + 2
    dma = pltpu.SemaphoreType.DMA
    return pl.pallas_call(
        lambda *refs: gather_kernel(levels, refs),
        out_shape=[
            jax.ShapeDtypeStruct((count * pair.shape[0], pair.shape[1] // 4), BF),
            shape(count * pack.shape[0], pack), shape(count * w_out.shape[0], w_out),
            shape(count * table.shape[0], table), shape(4 * tokens.shape[0], tokens), shape(4 * source.shape[0], source),
        ],
        in_specs=[ANY] * 6,
        out_specs=[ANY] * 6,
        scratch_shapes=[
            dma((jobs, Gather.sends(levels))), dma((jobs, count)),
            dma((GatherPair.sends(levels),)), dma((4 + 2 * levels,)),
            dma((6,)), dma((8,)), dma((3,)), dma((4,)), dma((6,)),
        ],
        compiler_params=pltpu.CompilerParams(collective_id=0, has_side_effects=True),
    )(pair, pack, w_out, table, tokens, source)


class Weights(Layer):
    w_o = property(lambda self: self.pack[:, 0:D])
    w_cq = property(lambda self: self.pack[:, D:2 * D])
    w_ckv = property(lambda self: self.pack[:, 2 * D:4 * D])
    w_co = property(lambda self: self.pack[:, 4 * D:5 * D])

    def w_in(self, units):
        return self.pack.at[:, 5 * D:5 * D + FF][:, units]

    def grad_in(self, units, value):
        self.grad_pack.at[:, 5 * D:5 * D + FF][:, units] = value

    def grad_out(self, units, value):
        self.grad_w_out[units, :] = value

    def grad_into(self, start, left, right):
        for step in range(right.shape[1] // SPAN):
            columns = slice(start + step * SPAN, start + (step + 1) * SPAN)
            self.grad_pack[:, columns] = dot_tn(left[...], right[:, step * SPAN:(step + 1) * SPAN]).astype(BF)


INS = ("w_pair", "pack", "w_out", "aux", "tokens_all", "source_all", "cotangent", "parents", "timestep")
OUTS = ("mixed", "grad_tokens", "source_grad", "grad_pair", "grad_pack", "grad_w_out", "table_part")


def layer_scratch(rows, tree, blocks):
    tiles = tree // SPAN
    plain = lambda *shape: pltpu.VMEM(shape, F32)
    short = lambda *shape: pltpu.VMEM(shape, BF)
    dma = pltpu.SemaphoreType.DMA
    return dict(
        mod=plain(8, 6 * D), mod_grad=plain(8, 6 * D), bias=plain(blocks, tree), corner=plain(SPAN, SPAN),
        h1=short(tree, D), q_masked=short(2, tree, 128), key=short(tree, 128), value=short(tree, 128),
        key_t=short(128, tree), value_t=short(2, HEAD + 16, tree),
        scores=plain(2, tree, SPAN), top=plain(2, 8, SPAN), mix=plain(2, HEAD + 16, SPAN),
        weights=short(tiles * (tiles + 1) // 2, 2, SPAN, SPAN), inverse=plain(2, 8, tree),
        attended_t=plain(128, tree), attended=short(tree, 128), gathered=short(rows, D),
        cross_k=short(4, 2 * ENC, 128), cross_v=short(4, 2 * ENC, 128), cross_q=short(rows, D), cross_p=plain(4, rows, 128),
        cross_out=short(rows, D), y1=plain(rows, D), y2=plain(rows, D), h2=short(rows, D), h3=short(rows, D),
        act=short(rows, FF), d_hidden=short(rows, FF), dy=plain(rows, D), db=short(rows, D), db1=short(rows, D),
        d_cross=plain(ENC, 2 * D), dcq=short(rows, D), d_attn=short(rows, D), d_att_all=short(tree, 128),
        d_masked=short(2, SPAN, 128), dq_t=plain(128, SPAN), dk=plain(tree, 128), dv=plain(tree, 128),
        d_pair=short(tree, 384), dh1_part=short(tree, D), dh1_box=short(4, rows, D),
        a_send=dma((tiles,)), a_recv=dma((tiles,)), d_send=dma((4,)), d_recv=dma((4,)), h_send=dma((tiles,)), h_recv=dma((tiles,)),
    )


def layer_kernel(levels, names, refs):
    place = Place(levels)
    refs = dict(zip(names, refs))
    refs["tokens_rows"] = refs["cotangent"].shape[0]
    w = Weights(place, refs)
    blk, leaf = place.blk, place.leaf
    peers = (place.near, place.far, place.opposite)
    barrier = pltpu.get_barrier_semaphore()
    for peer in peers:
        pl.semaphore_signal(barrier, inc=1, device_id=(leaf, peer), device_id_type=MESH)
    pl.semaphore_wait(barrier, 3)

    rows = w.tokens_rows
    tree = w.tokens_all.shape[0]
    tiles = tree // SPAN
    halves = rows // SPAN
    blocks = tree // BLOCK
    wide = 6 * D // (levels * 8)
    own_lanes = pl.ds(pl.multiple_of(blk * 128, 128), 128)

    read_modulation(w.aux, w.timestep[0], w.mod, wide)
    block_bias(w.parents, w.bias, blocks)
    row, column = iota((SPAN, SPAN), 0), iota((SPAN, SPAN), 1)
    same = (row < BLOCK) == (column < BLOCK)
    w.corner[...] = jnp.where(same & (row > column), -1e30, 0.0)
    w.mod_grad[...] = jnp.zeros_like(w.mod_grad)
    w.d_cross[...] = jnp.zeros_like(w.d_cross)
    w.dk[...] = jnp.zeros_like(w.dk)
    w.dv[...] = jnp.zeros_like(w.dv)
    loop(tiles, w.project)

    def attended_copy(tile, src):
        there = w.gathered.at[span(tile % halves), pl.ds(pl.multiple_of(src * 128, 128), 128)]
        return remote(w.attended.at[span(tile), :], there, w.a_send.at[tile], w.a_recv.at[src * halves + tile % halves], leaf, tile // halves)

    def forward(tile):
        w.attend(tile)
        away = tile // halves != blk
        pl.when(away)(lambda: attended_copy(tile, blk).start())

        def keep():
            w.gathered[span(tile % halves), own_lanes] = w.attended[span(tile), :]

        pl.when(jnp.logical_not(away))(keep)

    loop(tiles, forward)
    w.cross_keys()
    for peer in peers:
        for half in range(halves):
            attended_copy(blk * halves + half, peer).wait_recv()
    loop(halves, w.middle)
    loop(FF // SPAN, w.hidden)
    loop(halves, w.finish_forward)
    loop(halves, w.back_three)
    w.grad_into(4 * D, w.cross_out, w.db)
    loop(halves, w.back_cross)

    def da_copy(src, to):
        return remote(w.d_attn.at[:, pl.ds(pl.multiple_of(to * 128, 128), 128)], w.d_att_all.at[rows_of(src, rows), :],
                      w.d_send.at[to], w.d_recv.at[src], leaf, to)

    for peer in peers:
        da_copy(blk, peer).start()
    w.d_att_all[rows_of(blk, rows), :] = w.d_attn[:, own_lanes]
    w.grad_into(0, w.gathered, w.db1)
    w.grad_into(D, w.h2, w.dcq)
    low_cross = w.d_cross[...].astype(BF)
    for step in range(2 * D // SPAN):
        columns = slice(2 * D + step * SPAN, 2 * D + (step + 1) * SPAN)
        w.grad_pack[:, columns] = dot_tn(w.source_all[...], low_cross[:, step * SPAN:(step + 1) * SPAN]).astype(BF)
    w.source_grad[...] = dot_nt(low_cross, w.w_ckv)
    for peer in peers:
        da_copy(peer, peer).wait_recv()

    def part_copy(tile, src):
        there = w.dh1_box.at[src, span(tile % halves), :]
        return remote(w.dh1_part.at[span(tile), :], there, w.h_send.at[tile], w.h_recv.at[src * halves + tile % halves], leaf, tile // halves)

    def backward(step):
        tile = tiles - 1 - step
        w.attend_back(tile)
        pl.when(tile // halves != blk)(lambda: part_copy(tile, blk).start())

    loop(tiles, backward)

    def pair_grad(step):
        w.grad_pair[span(step), :] = dot_tn(w.h1[:, span(step)], w.d_pair[...]).astype(BF)

    loop(D // SPAN, pair_grad)
    for peer in peers:
        for half in range(halves):
            part_copy(blk * halves + half, peer).wait_recv()

    def last(chunk):
        here, own = span(chunk), span(blk * halves + chunk)
        dh1 = w.dh1_part[own, :].astype(F32)
        for peer in peers:
            dh1 = dh1 + w.dh1_box[peer, here, :].astype(F32)
        unit, root = unit_rows(w.tokens_all[own, :].astype(F32))
        w.sums(0, dh1, dh1 * unit)
        w.grad_tokens[here, :] = w.dy[here, :] + norm_back(dh1, unit, root, w.mod[0:1, D:2 * D])

    loop(halves, last)
    w.table_part[...] = table_payload(w.mod_grad[0:1, :], leaf, wide, levels * 8)

    def drain(tile):
        def gone():
            attended_copy(tile, blk).wait_send()
            part_copy(tile, blk).wait_send()

        pl.when(tile // halves != blk)(gone)

    loop(tiles, drain)
    for peer in peers:
        da_copy(blk, peer).wait_send()


def layer_all(levels, blocks, ins):
    rows, tree = ins["cotangent"].shape[0], ins["tokens_all"].shape[0]
    scratch = layer_scratch(rows, tree, blocks)
    outs = dict(
        mixed=((rows, D), BF), grad_tokens=((rows, D), F32), source_grad=((ENC, D), F32), grad_pair=((D, 384), BF),
        grad_pack=((D, 5 * D + FF), BF), grad_w_out=((FF, D), BF), table_part=((levels * 64, 128), F32),
    )
    names = INS + OUTS + tuple(scratch)
    return pl.pallas_call(
        lambda *refs: layer_kernel(levels, names, refs),
        out_shape=[jax.ShapeDtypeStruct(*outs[name]) for name in OUTS],
        in_specs=[SMEM if name in ("parents", "timestep") else VMEM for name in INS],
        out_specs=[VMEM] * len(OUTS),
        scratch_shapes=list(scratch.values()),
        compiler_params=pltpu.CompilerParams(collective_id=2, has_side_effects=True, vmem_limit_bytes=63 << 20),
    )(*[ins[name] for name in INS])


def reduce_kernel(levels, refs):
    (pair, pack, w_out, table, source, pair_out, pack_a, pack_b, w_out_out, table_out, source_out,
     pair_total, pack_total, out_total, table_total) = refs[:15]
    boxes, (send, recv, pair_send, pair_recv, settle_send, settle_recv, local, settle_box) = refs[15:-8], refs[-8:]
    moves = [(pair, pair_total), (pack, pack_total), (w_out, out_total), (table, table_total)]
    copies = [pltpu.make_async_copy(src, dst, local.at[n]) for n, (src, dst) in enumerate(moves)]
    for copy in copies:
        copy.start()
    place = Place(levels)
    place.greet()
    for copy in copies:
        copy.wait()

    def writer(out):
        def store(there, value):
            out[there, :] = value

        return store

    jobs = []
    count = levels * 8
    plan = [(out_total, slice(None), w_out_out), (pack_total, slice(*CUTS[0]), pack_a),
            (pack_total, slice(CUTS[1][0], sum(CUTS[1])), pack_b), (table_total, slice(None), table_out)]
    for n, (total, columns, out) in enumerate(plan):
        jobs.append(Reduce(place, total, total.shape[0] // count, columns, writer(out), boxes[5 * n:5 * n + 5], send.at[n], recv.at[n]))
    jobs.append(ReducePair(place, pair_total, pair_out, boxes[20:24], pair_send, pair_recv))
    jobs.append(Settle(place, source, source_out, settle_box, settle_send, settle_recv))
    run_all(jobs)
    for job in jobs:
        job.finish()


def reduce_all(levels, pair, pack, w_out, table, source):
    count = levels * 8
    dma = pltpu.SemaphoreType.DMA
    rows = pack.shape[0] // count
    out = lambda *shape: jax.ShapeDtypeStruct(shape, F32)
    boxes = []
    for each, width, kind in ((w_out.shape[0] // count, D, BF), (rows, CUTS[0][1], BF), (rows, CUTS[1][1], BF), (8, 128, F32)):
        boxes += Reduce.boxes(levels, each, width, kind)
    boxes += ReducePair.boxes(levels, rows, pair.shape[1], BF)
    return pl.pallas_call(
        lambda *refs: reduce_kernel(levels, refs),
        out_shape=[out(rows, 3 * D), out(rows, CUTS[0][1]), out(rows, CUTS[1][1]), out(w_out.shape[0] // count, D), out(8, 128),
                   out(source.shape[0] // 4, D)],
        in_specs=[ANY] * 4 + [VMEM],
        out_specs=[VMEM] * 6,
        scratch_shapes=[pltpu.VMEM(p.shape, p.dtype) for p in (pair, pack, w_out, table)] + boxes + [
            dma((4, Reduce.slots(levels))), dma((4, Reduce.slots(levels))),
            dma((ReducePair.slots(levels),)), dma((ReducePair.slots(levels),)), dma((4,)), dma((4,)), dma((4,)),
            pltpu.VMEM((source.shape[0], D), F32),
        ],
        compiler_params=pltpu.CompilerParams(collective_id=1, has_side_effects=True, vmem_limit_bytes=60 << 20),
    )(pair, pack, w_out, table, source)


def per_device(tokens, cotangent, encoded, parents, timestep, w_qkv, w_o, w_cq, w_ckv, w_co, w_in, w_out, mod_table):
    levels = lax.axis_size("leaf") // 2
    rows, wide = w_qkv.shape[0], mod_table.shape[1]
    pair = w_qkv.reshape(rows, 3, 4, 128).swapaxes(1, 2).reshape(rows, 3 * D)
    pack = jnp.concatenate((w_o, w_cq, w_ckv, w_co, w_in), axis=1)
    aux = jnp.concatenate(
        (
            jnp.pad(mod_table, ((0, 0), (0, 128 - wide))),
            jnp.full((64 - STEPS, 128), timestep[0], jnp.int32).astype(BF),
        ),
        axis=0,
    )
    w_pair, full_pack, full_out, full_aux, all_tokens, all_source = gather_all(levels, pair, pack, w_out, aux, tokens, encoded)
    ins = dict(
        w_pair=w_pair, pack=full_pack, w_out=full_out, aux=full_aux, tokens_all=all_tokens, source_all=all_source,
        cotangent=cotangent, parents=parents, timestep=timestep,
    )
    mixed, grad_tokens, source_part, pair_part, pack_part, out_part, table_part = layer_all(levels, parents.shape[1], ins)
    g_qkv, g_pack, g_in, g_out, table_sum, d_encoded = reduce_all(levels, pair_part, pack_part, out_part, table_part, source_part)
    steps_all = full_aux.reshape(-1, 64, 128)[::4, STEPS, 0].astype(jnp.int32)
    chosen = (jnp.arange(STEPS)[:, None] == steps_all[None, :]).astype(jnp.float32)
    table_grad = jnp.dot(chosen, table_sum[:, :wide], precision=PRECISE)
    return (
        mixed, grad_tokens, d_encoded, g_qkv, g_pack[:, :D], g_pack[:, D:2 * D], g_pack[:, 2 * D:4 * D],
        g_pack[:, 4 * D:5 * D], g_in, g_out, table_grad,
    )


def solution(mesh):
    fits = mesh.shape["blk"] == 4 and mesh.shape["leaf"] == 8
    return jax.shard_map(
        per_device if fits else generic_device,
        mesh=mesh,
        in_specs=(
            P(("leaf", "blk"), None),
            P(("leaf", "blk"), None),
            P(("leaf", "blk"), None),
            P("leaf", None),
            P("leaf"),
            P(("leaf", "blk"), None),
            P(("leaf", "blk"), None),
            P(("leaf", "blk"), None),
            P(("leaf", "blk"), None),
            P(("leaf", "blk"), None),
            P(("leaf", "blk"), None),
            P(("leaf", "blk"), None),
            P(None, ("leaf", "blk")),
        ),
        out_specs=(
            P(("leaf", "blk"), None),
            P(("leaf", "blk"), None),
            P(("leaf", "blk"), None),
            P(("leaf", "blk"), None),
            P(("leaf", "blk"), None),
            P(("leaf", "blk"), None),
            P(("leaf", "blk"), None),
            P(("leaf", "blk"), None),
            P(("leaf", "blk"), None),
            P(("leaf", "blk"), None),
            P(None, ("leaf", "blk")),
        ),
        check_vma=False,
    )
```

profile of v0, /device:TPU:0, one launch (start us, length us, event | category | flops | bytes accessed | tf_op | source)
XLA Modules:
  0.0 250.2 jit_solution(16957712687682212271)
XLA Ops:
  1.3 1.3 fusion.refs_3_
  2.6 0.8 reshape.39
  3.5 0.7 reshape.40.refs_0_
  4.1 0.7 constant_dynamic-update-slice_fusion.4
  4.9 0.7 constant_dynamic-update-slice_fusion.3
  5.6 0.8 constant_dynamic-update-slice_fusion.2
  6.3 0.7 constant_dynamic-update-slice_fusion.1
  7.1 0.8 constant_dynamic-update-slice_fusion.refs_1_
  7.9 0.7 copy-done.2
  8.6 58.0 %shard_map.212 = (bf16[512,384]{1,0:T(8,128)(2,1)}, bf16[512,4608]{1,0:T(8,128)(2,1)}, bf16[2048,512]{1,0:T(8,128)(2,1)}, bf16[2048,128]{1,0:T(8,128)(2,1)}, bf1...) custom-call(bf16[16,1536]{1,0:T(8,128)(2,1)} %reshape.40.refs_0_, bf16[16,4608]{1,0:T(8,128)(2,1)} %copy-done.2, ...), custom_call_target="tpu_custom_call" | custom-call | tf_op jit(solution)/shard_map/pallas_call | solution.py:1288
  66.6 114.5 %shard_map.213 = (bf16[512,512]{1,0:T(8,128)(2,1)}, f32[512,512]{1,0:T(8,128)}, f32[64,512]{1,0:T(8,128)}, bf16[512,384]{1,0:T(8,128)(2,1)}, bf16[512,4608]{1,0:...) custom-call(bf16[512,384]{1,0:T(8,128)(2,1)} %get-tuple-element.30.refs_0_, ...), custom_call_target="tpu_custom_call" | custom-call | tf_op jit(solution)/shard_map/pallas_call | solution.py:1478
  181.1 0.7 slice.22
  181.8 0.1 copy.28
  181.9 59.5 %shard_map.214 = (f32[16,1536]{1,0:T(8,128)}, f32[16,2560]{1,0:T(8,128)}, f32[16,2048]{1,0:T(8,128)}, f32[64,512]{1,0:T(8,128)}, f32[8,128]{1,0:T(8,128)}, /*index=5*/f32[16,512]{1,0:T(8,128)}) custom-call(bf16[512,384]{1,0:T(8,128)(2,1)} %get-tuple-element.38.refs_0_, bf16[512,4608]{1,0:T(8,128)(2,1)} %get-tuple-element.39.refs_1_, ...), custom_call_target="tpu_custom_call" | custom-call | tf_op jit(solution)/shard_map/pallas_call | solution.py:1529
  241.4 0.0 copy-start
  241.4 0.0 copy-start.6
  241.4 0.0 copy-start.5
  241.4 0.0 copy-start.4
  241.4 0.0 copy-start.3
  241.4 1.5 fusion.1
  243.0 1.5 slice.20
  244.5 1.4 fusion.4
  245.9 0.0 copy-done.1
  245.9 0.8 copy.42
  246.7 0.0 copy-done
  246.7 1.0 copy.43
  247.7 0.0 copy-done.6
  247.7 0.6 copy.44
  248.3 0.0 copy-done.5
  248.3 0.6 copy.45
  248.9 0.7 copy.46
  249.6 0.7 copy.47
  (6 shorter events, 0.0 us)
Async XLA Ops:
  7.9 0.7 copy-start.2
  181.9 64.0 %copy-start.1 = (bf16[512,512]{1,0:T(8,128)(2,1)S(1)}, bf16[512,512]{1,0:T(8,128)(2,1)}, u32[]{:S(2)}) copy-start(bf16[512,512]{1,0:T(8,128)(2,1)} %get-tuple-element.63) | copy-start | bytes 1572868
  241.4 5.3 %copy-start = (f32[512,512]{1,0:T(8,128)S(1)}, f32[512,512]{1,0:T(8,128)}, u32[]{:S(2)}) copy-start(f32[512,512]{1,0:T(8,128)} %get-tuple-element.64) | copy-start | bytes 3145732
  241.4 6.3 %copy-start.6 = (f32[16,512]{1,0:T(8,128)S(1)}, f32[16,512]{1,0:T(8,128)}, u32[]{:S(2)}) copy-start(f32[16,512]{1,0:T(8,128)} %get-tuple-element.65) | copy-start | bytes 98308
  241.4 6.9 %copy-start.5 = (f32[16,1536]{1,0:T(8,128)S(1)}, f32[16,1536]{1,0:T(8,128)}, u32[]{:S(2)}) copy-start(f32[16,1536]{1,0:T(8,128)} %get-tuple-element.66) | copy-start | bytes 294916
  241.4 7.5 %copy-start.4 = (f32[16,2048]{1,0:T(8,128)S(1)}, f32[16,2048]{1,0:T(8,128)}, u32[]{:S(2)}) copy-start(f32[16,2048]{1,0:T(8,128)} %get-tuple-element.71) | copy-start | bytes 393220
  241.4 8.1 %copy-start.3 = (f32[64,512]{1,0:T(8,128)S(1)}, f32[64,512]{1,0:T(8,128)}, u32[]{:S(2)}) copy-start(f32[64,512]{1,0:T(8,128)} %get-tuple-element.72) | copy-start | bytes 393220
where the time goes:
time: 255 us; the launch traced here: 250 us
  Pallas kernels  232 us (91%)
  local copies, waits for them, and re-layouts  14 us (5%)
    pallas_call x1, Pallas kernels, layer_all(): pl.pallas_call(lambda *refs: layer_kernel(levels, names, refs), out_shape...  115 us
    pallas_call x1, Pallas kernels, reduce_all(): pl.pallas_call(lambda *refs: reduce_kernel(levels, refs), out_shape=[out(...  59.5 us
    pallas_call x1, Pallas kernels, gather_all(): pl.pallas_call(lambda *refs: gather_kernel(levels, refs), out_shape=[jax....  58 us
    unnamed x25, local copies, waits for them, and re-layouts  8.03 us

commit v1 on v0

--- a/solution.py
+++ b/solution.py
@@ -416,17 +416,16 @@
     def greet(self):
         barrier = pltpu.get_barrier_semaphore()
 
+        count = self.levels * 2
+
         def hello(leaf, blk):
             pl.semaphore_signal(barrier, inc=1, device_id=(leaf, blk), device_id_type=MESH)
 
-        hello(self.sibling, self.blk)
-        hello(self.leaf, self.near)
-        hello(self.leaf, self.far)
-        hello(self.leaf, self.opposite)
-        pl.when(self.has_up)(lambda: hello(self.leaf + 2, self.blk))
-        pl.when(self.has_down)(lambda: hello(self.leaf - 2, self.blk))
-        ends = self.has_up.astype(jnp.int32) + self.has_down.astype(jnp.int32)
-        pl.semaphore_wait(barrier, 4 + ends)
+        for blk in (self.near, self.far, self.opposite):
+            hello(self.leaf, blk)
+        for step in range(1, count):
+            hello((self.leaf + step) % count, self.blk)
+        pl.semaphore_wait(barrier, count + 2)
 
 
 def remote(src, dst, send, recv, leaf, blk):
@@ -456,8 +455,8 @@
 
 
 class Gather:
-    def __init__(self, place, own, full, rows, columns, send_sem, recv_sem):
-        self.place, self.own, self.full, self.rows, self.columns = place, own, full, rows, columns
+    def __init__(self, place, full, rows, columns, send_sem, recv_sem):
+        self.place, self.full, self.rows, self.columns = place, full, rows, columns
         self.send_sem, self.recv_sem = send_sem, recv_sem
         self.sent = []
         self.count = 0
@@ -465,17 +464,14 @@
     def view(self, leaf, blk):
         return self.full.at[rows_of(leaf * 4 + blk, self.rows), self.columns]
 
-    def push(self, leaf, blk, targets, cond, own=False):
+    def push(self, leaf, blk, targets, cond):
         for to_leaf, to_blk, needs in targets:
             number = self.count
             self.count += 1
 
             def build(number=number, to_leaf=to_leaf, to_blk=to_blk):
                 there = self.view(leaf, blk)
-                return remote(
-                    self.own if own else there, there, self.send_sem.at[number],
-                    self.recv_sem.at[leaf * 4 + blk], to_leaf, to_blk,
-                )
+                return remote(there, there, self.send_sem.at[number], self.recv_sem.at[leaf * 4 + blk], to_leaf, to_blk)
 
             ok = both(cond, needs)
             under(ok, lambda: build().start())
@@ -503,10 +499,13 @@
 
     def steps(self):
         p = self.place
-        self.push(p.leaf, p.blk, self.to("first", "up", "down", "second", "sibling"), None, own=True)
+        self.push(p.leaf, p.blk, self.to("first", "up", "down", "sibling"), None)
         yield
         self.arrive(p.leaf, p.first)
-        self.push(p.leaf, p.first, self.to("up", "down", "second", "sibling"), None)
+        self.push(p.leaf, p.first, self.to("up", "down", "sibling"), None)
+        yield
+        self.push(p.leaf, p.blk, self.to("second"), None)
+        self.push(p.leaf, p.first, self.to("second"), None)
         yield
         for k in range(1, p.levels):
             below, above = p.leaf - 2 * k, p.leaf + 2 * k
@@ -542,26 +541,25 @@
 
 
 class Share:
-    def __init__(self, place, own, full, rows, send_sem, recv_sem):
-        self.place, self.own, self.full, self.rows = place, own, full, rows
+    def __init__(self, place, full, rows, send_sem, recv_sem):
+        self.place, self.full, self.rows = place, full, rows
         self.send_sem, self.recv_sem = send_sem, recv_sem
         self.half = rows // 2
 
     def view(self, blk, half):
         return self.full.at[pl.ds(pl.multiple_of(blk * self.rows + half * self.half, self.half), self.half), :]
 
-    def build(self, blk, half, to_blk, number, own=False):
+    def build(self, blk, half, to_blk, number):
         there = self.view(blk, half)
-        src = self.own.at[pl.ds(half * self.half, self.half), :] if own else there
-        return remote(src, there, self.send_sem.at[number], self.recv_sem.at[blk * 2 + half], self.place.leaf, to_blk)
+        return remote(there, there, self.send_sem.at[number], self.recv_sem.at[blk * 2 + half], self.place.leaf, to_blk)
 
     def steps(self):
         p = self.place
         self.copies = [
-            self.build(p.blk, 0, p.near, 0, True),
-            self.build(p.blk, 1, p.far, 1, True),
-            self.build(p.blk, 1, p.near, 2, True),
-            self.build(p.blk, 0, p.far, 3, True),
+            self.build(p.blk, 0, p.near, 0),
+            self.build(p.blk, 1, p.far, 1),
+            self.build(p.blk, 1, p.near, 2),
+            self.build(p.blk, 0, p.far, 3),
         ]
         for copy in self.copies:
             copy.start()
@@ -585,24 +583,24 @@
 
 
 class Spread:
-    def __init__(self, place, own, full, rows, send_sem, recv_sem):
-        self.place, self.own, self.full, self.rows = place, own, full, rows
+    def __init__(self, place, full, rows, send_sem, recv_sem):
+        self.place, self.full, self.rows = place, full, rows
         self.send_sem, self.recv_sem = send_sem, recv_sem
 
-    def build(self, src, blk, to_blk, number):
+    def build(self, blk, to_blk, number):
         there = self.full.at[rows_of(blk, self.rows), :]
-        return remote(there if src is None else src, there, self.send_sem.at[number], self.recv_sem.at[blk], self.place.leaf, to_blk)
+        return remote(there, there, self.send_sem.at[number], self.recv_sem.at[blk], self.place.leaf, to_blk)
 
     def start(self):
         p = self.place
-        self.copies = [self.build(self.own, p.blk, to, n) for n, to in enumerate((p.near, p.far, p.opposite))]
+        self.copies = [self.build(p.blk, to, n) for n, to in enumerate((p.near, p.far, p.opposite))]
         for copy in self.copies:
             copy.start()
 
     def arrive(self):
         p = self.place
         for blk in (p.near, p.far, p.opposite):
-            self.build(None, blk, p.near, 0).wait_recv()
+            self.build(blk, p.near, 0).wait_recv()
 
     def finish(self):
         for copy in self.copies:
@@ -612,7 +610,7 @@
 class Reduce:
     def __init__(self, place, total, rows, columns, out, boxes, send_sem, recv_sem):
         self.place, self.total, self.rows, self.columns, self.out = place, total, rows, columns, out
-        self.from_sibling, self.from_second, self.from_below, self.from_above, self.from_first = boxes
+        self.from_sibling, self.from_second, self.from_line, self.from_first = boxes
         self.send_sem, self.recv_sem = send_sem, recv_sem
         self.sent = []
 
@@ -625,8 +623,7 @@
         return [
             pltpu.VMEM((levels * 4 * rows, width), kind),
             pltpu.VMEM((levels * 2 * rows, width), kind),
-            pltpu.VMEM((levels * 2 * rows, width), kind),
-            pltpu.VMEM((levels * 2 * rows, width), kind),
+            pltpu.VMEM(((levels + 1) * 2 * rows, width), kind),
             pltpu.VMEM((rows, width), kind),
         ]
 
@@ -683,17 +680,20 @@
             for which, blk in enumerate((p.blk, p.first)):
                 up, down = 2 * (p.z + k) + which, 2 * (p.z - k) + which
 
+                here = 2 * p.levels + which if k == 0 else down
+                there = 2 * p.levels + which if k == 1 else down
+
                 def climb(up=up, blk=blk):
                     def more():
-                        self.arrived(self.from_below, up, 1, 3 * levels + up)
-                        self.add(p.leaf + 2 * k, blk, self.from_below, up)
+                        self.arrived(self.from_line, up, 1, 3 * levels + up)
+                        self.add(p.leaf + 2 * k, blk, self.from_line, up)
 
                     pl.when(p.has_down)(more)
 
-                def fall(down=down, blk=blk):
+                def fall(down=down, here=here, blk=blk):
                     def more():
-                        self.arrived(self.from_above, down, 1, 5 * levels + down)
-                        self.add(p.leaf - 2 * k, blk, self.from_above, down)
+                        self.arrived(self.from_line, here, 1, 5 * levels + down)
+                        self.add(p.leaf - 2 * k, blk, self.from_line, here)
 
                     pl.when(p.has_up)(more)
 
@@ -703,9 +703,9 @@
                 else:
                     can_up, can_down = p.z + k < levels, p.z >= k
                     under(can_up, climb)
-                    self.send(can_up, self.part(p.leaf + 2 * k, blk), self.from_below, up, 1, 3 * levels + up, p.leaf + 2, p.blk)
+                    self.send(can_up, self.part(p.leaf + 2 * k, blk), self.from_line, up, 1, 3 * levels + up, p.leaf + 2, p.blk)
                     under(can_down, fall)
-                    self.send(can_down, self.part(p.leaf - 2 * k, blk), self.from_above, down, 1, 5 * levels + down, p.leaf - 2, p.blk)
+                    self.send(can_down, self.part(p.leaf - 2 * k, blk), self.from_line, there, 1, 5 * levels + down, p.leaf - 2, p.blk)
             yield
         self.send(None, self.part(p.leaf, p.first), self.from_first, 0, 1, 7 * levels, p.leaf, p.first)
         yield
@@ -928,6 +928,100 @@
     def finish(self):
         for copy in self.copies:
             copy.wait_send()
+
+
+class TableSum:
+    def __init__(self, place, payload, box, rows_box, send_sem, recv_sem):
+        self.place, self.payload, self.box, self.rows_box = place, payload, box, rows_box
+        self.send_sem, self.recv_sem = send_sem, recv_sem
+        self.leaves = place.levels * 2
+        self.rows = self.leaves * 8
+
+    def first(self, src_blk, to_blk):
+        return remote(self.payload.at[rows_of(to_blk, self.rows), :], self.box.at[rows_of(src_blk, self.rows), :],
+                      self.send_sem.at[to_blk], self.recv_sem.at[src_blk], self.place.leaf, to_blk)
+
+    def second(self, src_leaf, to_leaf):
+        p = self.place
+        start = p.blk * self.leaves + to_leaf
+        return remote(self.payload.at[rows_of(start, 8), :], self.rows_box.at[rows_of(src_leaf, 8), :],
+                      self.send_sem.at[4 + to_leaf], self.recv_sem.at[4 + src_leaf], to_leaf, p.blk)
+
+    def steps(self):
+        p = self.place
+        peers = (p.near, p.far, p.opposite)
+        others = [(p.leaf + step) % self.leaves for step in range(1, self.leaves)]
+        for to in peers:
+            self.first(p.blk, to).start()
+        yield
+        here = rows_of(p.blk, self.rows)
+        total = self.payload[here, :]
+        for src in peers:
+            self.first(src, p.near).wait_recv()
+            total = total + self.box[rows_of(src, self.rows), :]
+        self.payload[here, :] = total
+        for to in others:
+            self.second(p.leaf, to).start()
+        self.rows_box[rows_of(p.leaf, 8), :] = self.payload[rows_of(p.blk * self.leaves + p.leaf, 8), :]
+        yield
+        for src in others:
+            self.second(src, others[0]).wait_recv()
+        yield
+
+    def finish(self):
+        p = self.place
+        for to in (p.near, p.far, p.opposite):
+            self.first(p.blk, to).wait_send()
+        for step in range(1, self.leaves):
+            self.second(p.leaf, (p.leaf + step) % self.leaves).wait_send()
+
+
+class TreeReduce:
+    def __init__(self, place, part, relay, box, send_sem, relay_sem, recv_sem):
+        self.place, self.part, self.relay, self.box = place, part, relay, box
+        self.send_sem, self.relay_sem, self.recv_sem = send_sem, relay_sem, recv_sem
+
+    def roles(self, tile):
+        owner, half = tile // 2, tile % 2
+        near, far = owner + 1 - 2 * (owner % 2), (owner + 2) % 4
+        direct, relayed = (near, far) if half == 0 else (far, near)
+        return owner, half, direct, relayed, 3 - owner
+
+    def to_owner(self, tile, which):
+        owner, half = tile // 2, tile % 2
+        return remote(self.part.at[span(tile), :], self.box.at[half, which], self.send_sem.at[tile],
+                      self.recv_sem.at[half * 2 + which], self.place.leaf, owner)
+
+    def to_relay(self, tile):
+        owner, half, direct, relayed, opposite = self.roles(tile)
+        return remote(self.part.at[span(tile), :], self.relay.at[half], self.send_sem.at[tile],
+                      self.relay_sem.at[half], self.place.leaf, relayed)
+
+    def offer(self, tile):
+        owner, half, direct, relayed, opposite = self.roles(tile)
+        pl.when(self.place.blk == opposite)(lambda: self.to_relay(tile).start())
+        pl.when(self.place.blk == direct)(lambda: self.to_owner(tile, 0).start())
+
+    def forward(self, tile):
+        owner, half, direct, relayed, opposite = self.roles(tile)
+
+        def go():
+            self.to_relay(tile).wait_recv()
+            total = self.part[span(tile), :].astype(F32) + self.relay[half].astype(F32)
+            self.part[span(tile), :] = total.astype(BF)
+            self.to_owner(tile, 1).start()
+
+        pl.when(self.place.blk == relayed)(go)
+
+    def arrive(self, half):
+        for which in range(2):
+            self.to_owner(half, which).wait_recv()
+
+    def finish(self, tile):
+        owner, half, direct, relayed, opposite = self.roles(tile)
+        pl.when(self.place.blk == opposite)(lambda: self.to_relay(tile).wait_send())
+        pl.when(self.place.blk == direct)(lambda: self.to_owner(tile, 0).wait_send())
+        pl.when(self.place.blk == relayed)(lambda: self.to_owner(tile, 1).wait_send())
 
 
 SPAN = 256
@@ -1008,7 +1102,7 @@
         )
 
 
-def table_payload(sums, leaf, wide, count):
+def table_payload(sums, wide, count):
     group = wide * 4
     offset = iota((count, group), 0) - shard_of_column(count, wide, group)
     held = jnp.zeros((count, group), F32)
@@ -1016,8 +1110,11 @@
         held = held + jnp.where(offset == 4 * part, sums[0:1, part * group:(part + 1) * group], 0.0)
     cut = lax.dot_general(held, spread_pattern(wide, group), (((1,), (1,)), ((), ())),
                           preferred_element_type=F32, precision=lax.Precision.HIGHEST)
+    leaves = count // 4
     row = iota((count * 8, count), 0)
-    chosen = (row == iota((count * 8, count), 1) * 8 + leaf).astype(F32)
+    tile = sum((row >= 8 * step).astype(jnp.int32) for step in range(1, count))
+    block = sum((row >= 8 * leaves * step).astype(jnp.int32) for step in range(1, 4))
+    chosen = (iota((count * 8, count), 1) == (tile - block * leaves) * 4 + block).astype(F32)
     return lax.dot_general(chosen, cut, (((1,), (0,)), ((), ())),
                            preferred_element_type=F32, precision=lax.Precision.HIGHEST)
 
@@ -1067,31 +1164,31 @@
         base = tile * (tile + 1) // 2
         self.top[...] = jnp.full_like(self.top, -3e30)
 
-        def score(j, diagonal):
-            keys = span(j)
+        def score(j, head, diagonal):
+            raw = dot_nt(self.key[span(j), :], self.q_masked[head, queries, :])
+            upper = raw[:BLOCK] + self.bias[pl.ds(2 * j, 1), queries]
+            lower = raw[BLOCK:] + self.bias[pl.ds(2 * j + 1, 1), queries]
+            kept = jnp.concatenate((upper, lower), axis=0)
+            return kept + self.corner[...] if diagonal else kept
+
+        def highest(j, diagonal):
             for head in range(2):
-                raw = dot_nt(self.key[keys, :], self.q_masked[head, queries, :])
-                upper = raw[:BLOCK] + self.bias[pl.ds(2 * j, 1), queries]
-                lower = raw[BLOCK:] + self.bias[pl.ds(2 * j + 1, 1), queries]
-                kept = jnp.concatenate((upper, lower), axis=0)
-                if diagonal:
-                    kept = kept + self.corner[...]
-                self.scores[head, keys, :] = kept
+                kept = score(j, head, diagonal)
                 self.top[head] = jnp.maximum(self.top[head], jnp.max(kept.reshape(SPAN // 8, 8, SPAN), axis=0))
 
-        loop(tile, lambda j: score(j, False))
-        score(tile, True)
+        loop(tile, lambda j: highest(j, False))
+        highest(tile, True)
         top = [jnp.max(self.top[head], axis=0, keepdims=True) for head in range(2)]
         self.mix[...] = jnp.zeros_like(self.mix)
 
-        def weigh(j):
-            keys = span(j)
+        def weigh(j, diagonal):
             for head in range(2):
-                weight = jnp.exp(self.scores[head, keys, :] - top[head]).astype(BF)
+                weight = jnp.exp(score(j, head, diagonal) - top[head]).astype(BF)
                 self.weights[base + j, head] = weight
-                self.mix[head] += dot(self.value_t[head, :, keys], weight)
-
-        loop(tile + 1, weigh)
+                self.mix[head] += dot(self.value_t[head, :, span(j)], weight)
+
+        loop(tile, lambda j: weigh(j, False))
+        weigh(tile, True)
         halves = []
         for head in range(2):
             inverse = 1.0 / self.mix[head, HEAD:HEAD + 8, :]
@@ -1113,8 +1210,7 @@
 
     def middle(self, chunk):
         rows = span(chunk)
-        own = span(self.place.blk * (self.tokens_rows // SPAN) + chunk)
-        y1 = self.tokens_all[own, :].astype(F32) + dot(self.gathered[rows, :], self.w_o)
+        y1 = self.tokens[rows, :].astype(F32) + dot(self.gathered[rows, :], self.w_o)
         self.y1[rows, :] = y1
         unit, root = unit_rows(y1)
         h2 = (unit * (1.0 + self.mod[0:1, 3 * D:4 * D]) + self.mod[0:1, 2 * D:3 * D]).astype(BF)
@@ -1130,7 +1226,7 @@
             right = jnp.max(jnp.where(lane >= ENC, raw, -3e38), axis=-1, keepdims=True)
             weight = jnp.exp(raw - jnp.where(lane < ENC, left, right))
             weight = weight / dot(weight.astype(BF), same)
-            self.cross_p[pair, rows, :] = weight
+            self.cross_p[pair, rows, :] = weight.astype(BF)
             out.append(dot(weight.astype(BF), self.cross_v[pair]))
         cross = jnp.concatenate(out, axis=1).astype(BF)
         self.cross_out[rows, :] = cross
@@ -1179,7 +1275,8 @@
         parts = []
         for pair in range(4):
             lanes = slice(128 * pair, 128 * pair + 128)
-            weight = self.cross_p[pair, rows, :]
+            low_weight = self.cross_p[pair, rows, :]
+            weight = low_weight.astype(F32)
             dc = dot_nt(dca[:, lanes], self.cross_v[pair])
             both_ = weight * dc
             left = jnp.sum(jnp.where(lane < ENC, both_, 0.0), axis=-1, keepdims=True)
@@ -1187,7 +1284,7 @@
             ds = (weight * (dc - jnp.where(lane < ENC, left, right))).astype(BF)
             parts.append((dot(ds, self.cross_k[pair]) * HEAD ** (-0.5)).astype(BF))
             dk = jnp.where(own, dot_tn(ds, self.cross_q[rows, lanes]), 0.0)
-            dv = jnp.where(own, dot_tn(weight.astype(BF), dca[:, lanes]), 0.0)
+            dv = jnp.where(own, dot_tn(low_weight, dca[:, lanes]), 0.0)
             self.d_cross[:, lanes] += dk[:ENC] + dk[ENC:]
             self.d_cross[:, 128 * pair + D:128 * pair + D + 128] += dv[:ENC] + dv[ENC:]
         dcq = jnp.concatenate(parts, axis=1)
@@ -1236,84 +1333,22 @@
         self.dh1_part[queries, :] = dot_nt(self.d_pair[queries, :], self.w_pair[...]).astype(BF)
 
 
-ANY = pl.BlockSpec(memory_space=pl.ANY)
 VMEM = pl.BlockSpec(memory_space=pltpu.VMEM)
 SMEM = pl.BlockSpec(memory_space=pltpu.SMEM)
-CUTS = ((0, 2560), (2560, FF))
-
-
-def gather_kernel(levels, refs):
-    (pair, pack, w_out, table, tokens, source, full_pair, full_pack, full_out, full_table, full_tokens, full_source,
-     send, recv, pair_send, pair_recv, share_send, share_recv, spread_send, spread_recv, local) = refs
-    place = Place(levels)
-    rows = pack.shape[0]
-    index = place.leaf * 4 + place.blk
-    pairs = [
-        (pack, full_pack.at[rows_of(index, rows), :]),
-        (w_out, full_out.at[rows_of(index, w_out.shape[0]), :]),
-        (table, full_table.at[rows_of(index, table.shape[0]), :]),
-        (tokens, full_tokens.at[rows_of(place.blk, tokens.shape[0]), :]),
-        (source, full_source.at[rows_of(place.blk, source.shape[0]), :]),
-    ]
-    weave = GatherPair(place, pair, full_pair, pair_send, pair_recv)
-    mine = weave.local(local.at[5])
-    mine.start()
-    locals_ = [pltpu.make_async_copy(src, dst, local.at[n]) for n, (src, dst) in enumerate(pairs)]
-    for copy in locals_:
-        copy.start()
-    place.greet()
-    mine.wait()
-    jobs = [Gather(place, table, full_table, table.shape[0], slice(None), send.at[0], recv.at[0])]
-    for n, (start, width) in enumerate(CUTS):
-        columns = pl.ds(start, width)
-        jobs.append(Gather(place, pack.at[:, columns], full_pack, rows, columns, send.at[n + 1], recv.at[n + 1]))
-    last = len(jobs)
-    jobs.append(Gather(place, w_out, full_out, w_out.shape[0], slice(None), send.at[last], recv.at[last]))
-    spread = Spread(place, source, full_source, source.shape[0], spread_send, spread_recv)
-    spread.start()
-    share = Share(place, tokens, full_tokens, tokens.shape[0], share_send, share_recv)
-    run_all([weave, share] + jobs)
-    spread.arrive()
-    for job in jobs + [share, spread, weave]:
-        job.finish()
-    for copy in locals_:
-        copy.wait()
-
-
-def gather_all(levels, pair, pack, w_out, table, tokens, source):
-    count = levels * 8
-    shape = lambda rows, like: jax.ShapeDtypeStruct((rows, like.shape[1]), like.dtype)
-    jobs = len(CUTS) + 2
-    dma = pltpu.SemaphoreType.DMA
-    return pl.pallas_call(
-        lambda *refs: gather_kernel(levels, refs),
-        out_shape=[
-            jax.ShapeDtypeStruct((count * pair.shape[0], pair.shape[1] // 4), BF),
-            shape(count * pack.shape[0], pack), shape(count * w_out.shape[0], w_out),
-            shape(count * table.shape[0], table), shape(4 * tokens.shape[0], tokens), shape(4 * source.shape[0], source),
-        ],
-        in_specs=[ANY] * 6,
-        out_specs=[ANY] * 6,
-        scratch_shapes=[
-            dma((jobs, Gather.sends(levels))), dma((jobs, count)),
-            dma((GatherPair.sends(levels),)), dma((4 + 2 * levels,)),
-            dma((6,)), dma((8,)), dma((3,)), dma((4,)), dma((6,)),
-        ],
-        compiler_params=pltpu.CompilerParams(collective_id=0, has_side_effects=True),
-    )(pair, pack, w_out, table, tokens, source)
+CROSS = 5 * D
 
 
 class Weights(Layer):
     w_o = property(lambda self: self.pack[:, 0:D])
     w_cq = property(lambda self: self.pack[:, D:2 * D])
     w_ckv = property(lambda self: self.pack[:, 2 * D:4 * D])
-    w_co = property(lambda self: self.pack[:, 4 * D:5 * D])
+    w_co = property(lambda self: self.pack[:, 4 * D:CROSS])
 
     def w_in(self, units):
-        return self.pack.at[:, 5 * D:5 * D + FF][:, units]
+        return self.pack.at[:, CROSS:CROSS + FF][:, units]
 
     def grad_in(self, units, value):
-        self.grad_pack.at[:, 5 * D:5 * D + FF][:, units] = value
+        self.grad_pack.at[:, CROSS:CROSS + FF][:, units] = value
 
     def grad_out(self, units, value):
         self.grad_w_out[units, :] = value
@@ -1324,86 +1359,184 @@
             self.grad_pack[:, columns] = dot_tn(left[...], right[:, step * SPAN:(step + 1) * SPAN]).astype(BF)
 
 
-INS = ("w_pair", "pack", "w_out", "aux", "tokens_all", "source_all", "cotangent", "parents", "timestep")
-OUTS = ("mixed", "grad_tokens", "source_grad", "grad_pair", "grad_pack", "grad_w_out", "table_part")
-
-
-def layer_scratch(rows, tree, blocks):
+INS = ("tokens", "cotangent", "encoded", "parents", "timestep", "i_qkv", "i_o", "i_cq", "i_ckv", "i_co", "i_in", "i_out", "aux_own")
+OUTS = ("mixed", "grad_tokens", "g_encoded", "g_qkv", "g_o", "g_cq", "g_ckv", "g_co", "g_in", "g_out", "g_table")
+
+
+def layer_scratch(rows, tree, blocks, levels, wide):
     tiles = tree // SPAN
+    count = levels * 8
+    each = D // count
     plain = lambda *shape: pltpu.VMEM(shape, F32)
     short = lambda *shape: pltpu.VMEM(shape, BF)
     dma = pltpu.SemaphoreType.DMA
-    return dict(
+    scratch = dict(
+        pair_own=short(each, 3 * D), w_pair=short(D, 384), pack=short(D, CROSS + FF), w_out=short(FF, D),
+        aux=short(count * 64, 128), tokens_all=short(tree, D), source_all=short(ENC, D),
         mod=plain(8, 6 * D), mod_grad=plain(8, 6 * D), bias=plain(blocks, tree), corner=plain(SPAN, SPAN),
         h1=short(tree, D), q_masked=short(2, tree, 128), key=short(tree, 128), value=short(tree, 128),
         key_t=short(128, tree), value_t=short(2, HEAD + 16, tree),
-        scores=plain(2, tree, SPAN), top=plain(2, 8, SPAN), mix=plain(2, HEAD + 16, SPAN),
+        top=plain(2, 8, SPAN), mix=plain(2, HEAD + 16, SPAN),
         weights=short(tiles * (tiles + 1) // 2, 2, SPAN, SPAN), inverse=plain(2, 8, tree),
         attended_t=plain(128, tree), attended=short(tree, 128), gathered=short(rows, D),
-        cross_k=short(4, 2 * ENC, 128), cross_v=short(4, 2 * ENC, 128), cross_q=short(rows, D), cross_p=plain(4, rows, 128),
-        cross_out=short(rows, D), y1=plain(rows, D), y2=plain(rows, D), h2=short(rows, D), h3=short(rows, D),
-        act=short(rows, FF), d_hidden=short(rows, FF), dy=plain(rows, D), db=short(rows, D), db1=short(rows, D),
-        d_cross=plain(ENC, 2 * D), dcq=short(rows, D), d_attn=short(rows, D), d_att_all=short(tree, 128),
+        cross_k=short(4, 2 * ENC, 128), cross_v=short(4, 2 * ENC, 128), cross_q=short(rows, D), cross_p=short(4, rows, 128),
+        cross_out=short(rows, D), y1=plain(rows, D), h2=short(rows, D), h3=short(rows, D),
+        act=short(rows, FF), d_hidden=short(rows, FF),
+        d_cross=plain(ENC, 2 * D), dcq=short(rows, D), d_att_all=short(tree, 128),
         d_masked=short(2, SPAN, 128), dq_t=plain(128, SPAN), dk=plain(tree, 128), dv=plain(tree, 128),
-        d_pair=short(tree, 384), dh1_part=short(tree, D), dh1_box=short(4, rows, D),
-        a_send=dma((tiles,)), a_recv=dma((tiles,)), d_send=dma((4,)), d_recv=dma((4,)), h_send=dma((tiles,)), h_recv=dma((tiles,)),
-    )
-
-
-def layer_kernel(levels, names, refs):
+        d_pair=short(tree, 384), relay=short(2, SPAN, D), dh1_box=short(2, 2, SPAN, D),
+        grad_pack=short(D, CROSS + FF), grad_w_out=short(FF, D), grad_pair=short(D, 384), source_part=plain(ENC, D),
+        payload=plain(count * 8, 128), table_box=plain(count * 8, 128), table_rows=plain(levels * 16, 128), settle_box=plain(ENC, D),
+        a_send=dma((tiles,)), a_recv=dma((tiles,)), d_send=dma((4,)), d_recv=dma((4,)),
+        h_send=dma((tiles,)), h_relay=dma((2,)), h_recv=dma((4,)),
+        send=dma((4, Gather.sends(levels))), recv=dma((4, count)),
+        pair_send=dma((GatherPair.sends(levels),)), pair_recv=dma((4 + 2 * levels,)),
+        share_send=dma((6,)), share_recv=dma((8,)), spread_send=dma((3,)), spread_recv=dma((4,)),
+        r_send=dma((3, Reduce.slots(levels))), r_recv=dma((3, Reduce.slots(levels))),
+        rp_send=dma((ReducePair.slots(levels),)), rp_recv=dma((ReducePair.slots(levels),)),
+        settle_send=dma((4,)), settle_recv=dma((4,)), t_send=dma((4 + 2 * levels,)), t_recv=dma((4 + 2 * levels,)),
+    )
+    for name, height, width in (("box_out", FF // count, D), ("box_in", each, FF), ("box_cross", each, CROSS)):
+        for n, box in enumerate(Reduce.boxes(levels, height, width, BF)):
+            scratch[f"{name}{n}"] = box
+    for n, box in enumerate(ReducePair.boxes(levels, each, 384, BF)):
+        scratch[f"box_pair{n}"] = box
+    return scratch
+
+
+def layer_kernel(levels, wide, names, refs):
     place = Place(levels)
     refs = dict(zip(names, refs))
-    refs["tokens_rows"] = refs["cotangent"].shape[0]
+    refs["y2"] = refs["dy"] = refs["grad_tokens"]
+    refs["db"] = refs["db1"] = refs["h3"]
+    refs["d_attn"] = refs["cross_q"]
+    refs["dh1_part"] = refs["tokens_all"]
     w = Weights(place, refs)
     blk, leaf = place.blk, place.leaf
     peers = (place.near, place.far, place.opposite)
-    barrier = pltpu.get_barrier_semaphore()
-    for peer in peers:
-        pl.semaphore_signal(barrier, inc=1, device_id=(leaf, peer), device_id_type=MESH)
-    pl.semaphore_wait(barrier, 3)
-
-    rows = w.tokens_rows
+    rows = w.tokens.shape[0]
     tree = w.tokens_all.shape[0]
     tiles = tree // SPAN
     halves = rows // SPAN
     blocks = tree // BLOCK
-    wide = 6 * D // (levels * 8)
+    count = levels * 8
+    each = D // count
+    index = leaf * 4 + blk
     own_lanes = pl.ds(pl.multiple_of(blk * 128, 128), 128)
 
-    read_modulation(w.aux, w.timestep[0], w.mod, wide)
-    block_bias(w.parents, w.bias, blocks)
-    row, column = iota((SPAN, SPAN), 0), iota((SPAN, SPAN), 1)
-    same = (row < BLOCK) == (column < BLOCK)
-    w.corner[...] = jnp.where(same & (row > column), -1e30, 0.0)
+    w.tokens_all[rows_of(blk, rows), :] = w.tokens[...]
+    w.source_all[rows_of(blk, w.encoded.shape[0]), :] = w.encoded[...]
+    mine = rows_of(index, each)
+    start = 0
+    for name in ("i_o", "i_cq", "i_ckv", "i_co", "i_in"):
+        width = refs[name].shape[1]
+        w.pack[mine, start:start + width] = refs[name][...]
+        start += width
+    w.w_out[rows_of(index, w.i_out.shape[0]), :] = w.i_out[...]
+    w.aux[rows_of(index, 64), :] = w.aux_own[...]
+    for pair in range(4):
+        for third in range(3):
+            w.pair_own[:, 384 * pair + 128 * third:384 * pair + 128 * third + 128] = (
+                w.i_qkv[:, D * third + 128 * pair:D * third + 128 * pair + 128])
+    w.w_pair[mine, :] = w.pair_own[:, pl.ds(pl.multiple_of(blk * 384, 128), 384)]
+    place.greet()
+
+    weave = GatherPair(place, w.pair_own, w.w_pair, w.pair_send, w.pair_recv)
+    table = Gather(place, w.aux, 64, slice(None), w.send.at[0], w.recv.at[0])
+    share = Share(place, w.tokens_all, rows, w.share_send, w.share_recv)
+    spread = Spread(place, w.source_all, w.encoded.shape[0], w.spread_send, w.spread_recv)
+    loads = [
+        Gather(place, w.pack, each, slice(0, CROSS), w.send.at[1], w.recv.at[1]),
+        Gather(place, w.pack, each, slice(CROSS, CROSS + FF), w.send.at[2], w.recv.at[2]),
+        Gather(place, w.w_out, FF // count, slice(None), w.send.at[3], w.recv.at[3]),
+    ]
+    weave_steps, table_steps, share_steps = weave.steps(), table.steps(), share.steps()
+    load_steps = [load.steps() for load in loads]
+
+    def ticks(steps, number=1):
+        for turn in range(number):
+            for step in steps:
+                next(step, None)
+
+    ticks([weave_steps, table_steps, share_steps])
+    spread.start()
+    ticks(load_steps)
     w.mod_grad[...] = jnp.zeros_like(w.mod_grad)
     w.d_cross[...] = jnp.zeros_like(w.d_cross)
     w.dk[...] = jnp.zeros_like(w.dk)
     w.dv[...] = jnp.zeros_like(w.dv)
-    loop(tiles, w.project)
+    block_bias(w.parents, w.bias, blocks)
+    row, column = iota((SPAN, SPAN), 0), iota((SPAN, SPAN), 1)
+    w.corner[...] = jnp.where(((row < BLOCK) == (column < BLOCK)) & (row > column), -1e30, 0.0)
+    ticks([weave_steps, table_steps], 2)
+    ticks([share_steps])
+    ticks(load_steps)
+    ticks([weave_steps, table_steps], 10)
+    read_modulation(w.aux, w.timestep[0], w.mod, wide)
+
+    def project(block):
+        for half in range(halves):
+            w.project(block * halves + half)
+
+    project(blk)
+    ticks(load_steps)
+    ticks([share_steps])
+    project(place.near)
+    project(place.far)
+    ticks([share_steps])
+    project(place.opposite)
+    ticks(load_steps)
 
     def attended_copy(tile, src):
         there = w.gathered.at[span(tile % halves), pl.ds(pl.multiple_of(src * 128, 128), 128)]
         return remote(w.attended.at[span(tile), :], there, w.a_send.at[tile], w.a_recv.at[src * halves + tile % halves], leaf, tile // halves)
 
-    def forward(tile):
+    for tile in range(tiles):
         w.attend(tile)
         away = tile // halves != blk
-        pl.when(away)(lambda: attended_copy(tile, blk).start())
-
-        def keep():
+        pl.when(away)(lambda tile=tile: attended_copy(tile, blk).start())
+
+        def keep(tile=tile):
             w.gathered[span(tile % halves), own_lanes] = w.attended[span(tile), :]
 
         pl.when(jnp.logical_not(away))(keep)
-
-    loop(tiles, forward)
+        ticks(load_steps)
+    ticks(load_steps, 20)
+    spread.arrive()
     w.cross_keys()
     for peer in peers:
         for half in range(halves):
             attended_copy(blk * halves + half, peer).wait_recv()
     loop(halves, w.middle)
     loop(FF // SPAN, w.hidden)
+    for job in loads + [weave, table, share, spread]:
+        job.finish()
+
+    def boxes(name, number=4):
+        return [refs[f"{name}{n}"] for n in range(number)]
+
+    def store_out(there, value):
+        w.g_out[there, :] = value
+
+    def store_in(there, value):
+        w.g_in[there, :] = value
+
+    def store_cross(there, value):
+        w.g_o[there, :] = value[:, 0:D]
+        w.g_cq[there, :] = value[:, D:2 * D]
+        w.g_ckv[there, :] = value[:, 2 * D:4 * D]
+        w.g_co[there, :] = value[:, 4 * D:5 * D]
+
+    sums = [
+        Reduce(place, w.grad_w_out, FF // count, slice(None), store_out, boxes("box_out"), w.r_send.at[0], w.r_recv.at[0]),
+        Reduce(place, w.grad_pack, each, slice(CROSS, CROSS + FF), store_in, boxes("box_in"), w.r_send.at[1], w.r_recv.at[1]),
+    ]
+    sum_steps = [job.steps() for job in sums]
+    ticks(sum_steps)
     loop(halves, w.finish_forward)
+    ticks(sum_steps)
     loop(halves, w.back_three)
+    ticks(sum_steps)
     w.grad_into(4 * D, w.cross_out, w.db)
     loop(halves, w.back_cross)
 
@@ -1414,138 +1547,80 @@
     for peer in peers:
         da_copy(blk, peer).start()
     w.d_att_all[rows_of(blk, rows), :] = w.d_attn[:, own_lanes]
+    ticks(sum_steps)
     w.grad_into(0, w.gathered, w.db1)
     w.grad_into(D, w.h2, w.dcq)
     low_cross = w.d_cross[...].astype(BF)
     for step in range(2 * D // SPAN):
         columns = slice(2 * D + step * SPAN, 2 * D + (step + 1) * SPAN)
         w.grad_pack[:, columns] = dot_tn(w.source_all[...], low_cross[:, step * SPAN:(step + 1) * SPAN]).astype(BF)
-    w.source_grad[...] = dot_nt(low_cross, w.w_ckv)
+    w.source_part[...] = dot_nt(low_cross, w.w_ckv)
+    sums.append(Reduce(place, w.grad_pack, each, slice(0, CROSS), store_cross, boxes("box_cross"), w.r_send.at[2], w.r_recv.at[2]))
+    settle = Settle(place, w.source_part, w.g_encoded, w.settle_box, w.settle_send, w.settle_recv)
+    later_steps = [sums[2].steps(), settle.steps()]
+    ticks(later_steps)
     for peer in peers:
         da_copy(peer, peer).wait_recv()
 
-    def part_copy(tile, src):
-        there = w.dh1_box.at[src, span(tile % halves), :]
-        return remote(w.dh1_part.at[span(tile), :], there, w.h_send.at[tile], w.h_recv.at[src * halves + tile % halves], leaf, tile // halves)
-
-    def backward(step):
-        tile = tiles - 1 - step
+    tree_sum = TreeReduce(place, w.dh1_part, w.relay, w.dh1_box, w.h_send, w.h_relay, w.h_recv)
+    for tile in range(tiles - 1, -1, -1):
         w.attend_back(tile)
-        pl.when(tile // halves != blk)(lambda: part_copy(tile, blk).start())
-
-    loop(tiles, backward)
+        tree_sum.offer(tile)
+        if tile + 1 < tiles:
+            tree_sum.forward(tile + 1)
+        ticks(sum_steps)
+        ticks(later_steps)
+    tree_sum.forward(0)
 
     def pair_grad(step):
         w.grad_pair[span(step), :] = dot_tn(w.h1[:, span(step)], w.d_pair[...]).astype(BF)
 
     loop(D // SPAN, pair_grad)
-    for peer in peers:
-        for half in range(halves):
-            part_copy(blk * halves + half, peer).wait_recv()
-
-    def last(chunk):
-        here, own = span(chunk), span(blk * halves + chunk)
-        dh1 = w.dh1_part[own, :].astype(F32)
-        for peer in peers:
-            dh1 = dh1 + w.dh1_box[peer, here, :].astype(F32)
-        unit, root = unit_rows(w.tokens_all[own, :].astype(F32))
+    pair_sum = ReducePair(place, w.grad_pair, w.g_qkv, boxes("box_pair", 4), w.rp_send, w.rp_recv)
+    pair_steps = pair_sum.steps()
+    ticks([pair_steps])
+    ticks(sum_steps + later_steps, 10)
+    ticks([pair_steps], 3)
+
+    def last(half):
+        tree_sum.arrive(half)
+        here, own = span(half), span(blk * halves + half)
+        dh1 = w.dh1_part[own, :].astype(F32) + w.dh1_box[half, 0].astype(F32) + w.dh1_box[half, 1].astype(F32)
+        unit, root = unit_rows(w.tokens[here, :].astype(F32))
         w.sums(0, dh1, dh1 * unit)
         w.grad_tokens[here, :] = w.dy[here, :] + norm_back(dh1, unit, root, w.mod[0:1, D:2 * D])
 
-    loop(halves, last)
-    w.table_part[...] = table_payload(w.mod_grad[0:1, :], leaf, wide, levels * 8)
-
-    def drain(tile):
-        def gone():
-            attended_copy(tile, blk).wait_send()
-            part_copy(tile, blk).wait_send()
-
-        pl.when(tile // halves != blk)(gone)
-
-    loop(tiles, drain)
+    for half in range(halves):
+        last(half)
+    w.payload[...] = table_payload(w.mod_grad[0:1, :], wide, count)
+    table_sum = TableSum(place, w.payload, w.table_box, w.table_rows, w.t_send, w.t_recv)
+    ticks([table_sum.steps(), pair_steps], 0)
+    table_steps = table_sum.steps()
+    ticks([table_steps, pair_steps], 10)
+
+    leaves = levels * 2
+    chosen = (iota((leaves, count * 64), 1) == iota((leaves, count * 64), 0) * 256 + STEPS).astype(BF)
+    steps_all = dot(chosen, w.aux[...])
+    line = iota((64, 128), 0).astype(F32)
+    grad_table = jnp.zeros((64, 128), F32)
+    for tree_at in range(leaves):
+        grad_table = grad_table + jnp.where(line == steps_all[tree_at:tree_at + 1, :], w.table_rows[8 * tree_at:8 * tree_at + 1, :], 0.0)
+    w.g_table[...] = grad_table[:STEPS, :wide]
+
+    for tile in range(tiles):
+        pl.when(tile // halves != blk)(lambda tile=tile: attended_copy(tile, blk).wait_send())
+        tree_sum.finish(tile)
     for peer in peers:
         da_copy(blk, peer).wait_send()
-
-
-def layer_all(levels, blocks, ins):
-    rows, tree = ins["cotangent"].shape[0], ins["tokens_all"].shape[0]
-    scratch = layer_scratch(rows, tree, blocks)
-    outs = dict(
-        mixed=((rows, D), BF), grad_tokens=((rows, D), F32), source_grad=((ENC, D), F32), grad_pair=((D, 384), BF),
-        grad_pack=((D, 5 * D + FF), BF), grad_w_out=((FF, D), BF), table_part=((levels * 64, 128), F32),
-    )
-    names = INS + OUTS + tuple(scratch)
-    return pl.pallas_call(
-        lambda *refs: layer_kernel(levels, names, refs),
-        out_shape=[jax.ShapeDtypeStruct(*outs[name]) for name in OUTS],
-        in_specs=[SMEM if name in ("parents", "timestep") else VMEM for name in INS],
-        out_specs=[VMEM] * len(OUTS),
-        scratch_shapes=list(scratch.values()),
-        compiler_params=pltpu.CompilerParams(collective_id=2, has_side_effects=True, vmem_limit_bytes=63 << 20),
-    )(*[ins[name] for name in INS])
-
-
-def reduce_kernel(levels, refs):
-    (pair, pack, w_out, table, source, pair_out, pack_a, pack_b, w_out_out, table_out, source_out,
-     pair_total, pack_total, out_total, table_total) = refs[:15]
-    boxes, (send, recv, pair_send, pair_recv, settle_send, settle_recv, local, settle_box) = refs[15:-8], refs[-8:]
-    moves = [(pair, pair_total), (pack, pack_total), (w_out, out_total), (table, table_total)]
-    copies = [pltpu.make_async_copy(src, dst, local.at[n]) for n, (src, dst) in enumerate(moves)]
-    for copy in copies:
-        copy.start()
-    place = Place(levels)
-    place.greet()
-    for copy in copies:
-        copy.wait()
-
-    def writer(out):
-        def store(there, value):
-            out[there, :] = value
-
-        return store
-
-    jobs = []
-    count = levels * 8
-    plan = [(out_total, slice(None), w_out_out), (pack_total, slice(*CUTS[0]), pack_a),
-            (pack_total, slice(CUTS[1][0], sum(CUTS[1])), pack_b), (table_total, slice(None), table_out)]
-    for n, (total, columns, out) in enumerate(plan):
-        jobs.append(Reduce(place, total, total.shape[0] // count, columns, writer(out), boxes[5 * n:5 * n + 5], send.at[n], recv.at[n]))
-    jobs.append(ReducePair(place, pair_total, pair_out, boxes[20:24], pair_send, pair_recv))
-    jobs.append(Settle(place, source, source_out, settle_box, settle_send, settle_recv))
-    run_all(jobs)
-    for job in jobs:
+    for job in sums + [settle, pair_sum, table_sum]:
         job.finish()
-
-
-def reduce_all(levels, pair, pack, w_out, table, source):
-    count = levels * 8
-    dma = pltpu.SemaphoreType.DMA
-    rows = pack.shape[0] // count
-    out = lambda *shape: jax.ShapeDtypeStruct(shape, F32)
-    boxes = []
-    for each, width, kind in ((w_out.shape[0] // count, D, BF), (rows, CUTS[0][1], BF), (rows, CUTS[1][1], BF), (8, 128, F32)):
-        boxes += Reduce.boxes(levels, each, width, kind)
-    boxes += ReducePair.boxes(levels, rows, pair.shape[1], BF)
-    return pl.pallas_call(
-        lambda *refs: reduce_kernel(levels, refs),
-        out_shape=[out(rows, 3 * D), out(rows, CUTS[0][1]), out(rows, CUTS[1][1]), out(w_out.shape[0] // count, D), out(8, 128),
-                   out(source.shape[0] // 4, D)],
-        in_specs=[ANY] * 4 + [VMEM],
-        out_specs=[VMEM] * 6,
-        scratch_shapes=[pltpu.VMEM(p.shape, p.dtype) for p in (pair, pack, w_out, table)] + boxes + [
-            dma((4, Reduce.slots(levels))), dma((4, Reduce.slots(levels))),
-            dma((ReducePair.slots(levels),)), dma((ReducePair.slots(levels),)), dma((4,)), dma((4,)), dma((4,)),
-            pltpu.VMEM((source.shape[0], D), F32),
-        ],
-        compiler_params=pltpu.CompilerParams(collective_id=1, has_side_effects=True, vmem_limit_bytes=60 << 20),
-    )(pair, pack, w_out, table, source)
 
 
 def per_device(tokens, cotangent, encoded, parents, timestep, w_qkv, w_o, w_cq, w_ckv, w_co, w_in, w_out, mod_table):
     levels = lax.axis_size("leaf") // 2
-    rows, wide = w_qkv.shape[0], mod_table.shape[1]
-    pair = w_qkv.reshape(rows, 3, 4, 128).swapaxes(1, 2).reshape(rows, 3 * D)
-    pack = jnp.concatenate((w_o, w_cq, w_ckv, w_co, w_in), axis=1)
+    rows, wide = tokens.shape[0], mod_table.shape[1]
+    blocks = parents.shape[1]
+    tree = blocks * BLOCK
     aux = jnp.concatenate(
         (
             jnp.pad(mod_table, ((0, 0), (0, 128 - wide))),
@@ -1553,20 +1628,19 @@
         ),
         axis=0,
     )
-    w_pair, full_pack, full_out, full_aux, all_tokens, all_source = gather_all(levels, pair, pack, w_out, aux, tokens, encoded)
-    ins = dict(
-        w_pair=w_pair, pack=full_pack, w_out=full_out, aux=full_aux, tokens_all=all_tokens, source_all=all_source,
-        cotangent=cotangent, parents=parents, timestep=timestep,
-    )
-    mixed, grad_tokens, source_part, pair_part, pack_part, out_part, table_part = layer_all(levels, parents.shape[1], ins)
-    g_qkv, g_pack, g_in, g_out, table_sum, d_encoded = reduce_all(levels, pair_part, pack_part, out_part, table_part, source_part)
-    steps_all = full_aux.reshape(-1, 64, 128)[::4, STEPS, 0].astype(jnp.int32)
-    chosen = (jnp.arange(STEPS)[:, None] == steps_all[None, :]).astype(jnp.float32)
-    table_grad = jnp.dot(chosen, table_sum[:, :wide], precision=PRECISE)
-    return (
-        mixed, grad_tokens, d_encoded, g_qkv, g_pack[:, :D], g_pack[:, D:2 * D], g_pack[:, 2 * D:4 * D],
-        g_pack[:, 4 * D:5 * D], g_in, g_out, table_grad,
-    )
+    ins = (tokens, cotangent, encoded, parents, timestep, w_qkv, w_o, w_cq, w_ckv, w_co, w_in, w_out, aux)
+    scratch = layer_scratch(rows, tree, blocks, levels, wide)
+    out = lambda like: jax.ShapeDtypeStruct(like.shape, F32)
+    names = INS + OUTS + tuple(scratch)
+    return pl.pallas_call(
+        lambda *refs: layer_kernel(levels, wide, names, refs),
+        out_shape=[jax.ShapeDtypeStruct((rows, D), BF), out(tokens), out(encoded)]
+        + [out(weight) for weight in (w_qkv, w_o, w_cq, w_ckv, w_co, w_in, w_out, mod_table)],
+        in_specs=[SMEM if name in ("parents", "timestep") else VMEM for name in INS],
+        out_specs=[VMEM] * len(OUTS),
+        scratch_shapes=list(scratch.values()),
+        compiler_params=pltpu.CompilerParams(collective_id=0, has_side_effects=True, vmem_limit_bytes=(64 << 20) - (64 << 10)),
+    )(*ins)
 
 
 def solution(mesh):

time: 255 us -> 218 us (0.85); the launches traced: 250 us -> 217 us
  Pallas kernels: 232 us -> 206 us
  local copies, waits for them, and re-layouts: 14 us -> 9.23 us
    pallas_call x3 -> x1, Pallas kernels: 232 us -> 206 us  [per_device(): pl.pallas_call(lambda *refs: layer_kernel(levels, wide, names, refs), out...]
    slice x3 -> x0, local copies, waits for them, and re-layouts: 3.63 us -> none  [the longest x1 1.47 us: per_device(): g_pack[:, 2 * D:4 * D]]
    unnamed x25 -> x31, local copies, waits for them, and re-layouts: 8.03 us -> 9.23 us
where the time goes in v1:
time: 218 us; the launch traced here: 217 us
  Pallas kernels  206 us (94%)
  local copies, waits for them, and re-layouts  9.23 us (4%)
    pallas_call x1, Pallas kernels, per_device(): pl.pallas_call(lambda *refs: layer_kernel(levels, wide, names, refs), out...  206 us
    unnamed x31, local copies, waits for them, and re-layouts  9.23 us

profile of v1, /device:TPU:0, one launch (start us, length us, event | category | flops | bytes accessed | tf_op | source)
XLA Modules:
  0.0 217.5 jit_solution(14034408497494988132)
XLA Ops:
  1.3 1.3 fusion.refs_12_
  2.6 205.6 %shard_map.212 = (bf16[512,512]{1,0:T(8,128)(2,1)}, f32[512,512]{1,0:T(8,128)}, f32[16,512]{1,0:T(8,128)}, f32[16,1536]{1,0:T(8,128)}, f32[16,512]{1,0:T(8,128)}...) custom-call(bf16[512,512]{1,0:T(8,128)(2,1)} %refs_0_.1, ...), custom_call_target="tpu_custom_call" | custom-call | tf_op jit(solution)/shard_map/pallas_call | solution.py:1635
  208.2 0.0 copy-start
  208.2 2.0 copy.36
  210.2 0.0 copy-done
  210.2 0.0 copy-start.8
  210.2 0.0 copy-start.3
  210.2 1.0 copy.37
  211.2 0.0 copy-done.8
  211.2 0.6 copy.38
  211.8 0.0 copy-done.3
  211.8 0.0 copy-start.7
  211.8 0.0 copy-start.6
  211.8 0.6 copy.39
  212.4 0.1 copy-done.7
  212.5 0.0 copy-start.4
  212.5 0.6 copy.40
  213.2 0.0 copy-done.6
  213.2 0.0 copy-start.2
  213.2 0.6 copy.41
  213.8 0.0 copy-done.4
  213.8 0.0 copy-start.5
  213.8 0.6 copy.42
  214.4 0.1 copy-done.5
  214.5 0.6 copy.43
  215.2 0.0 copy-done.2
  215.2 0.0 copy-start.1
  215.2 0.7 copy.44
  215.8 0.3 copy-done.1
  216.1 0.7 copy.45
  216.8 0.1 copy-done.9
  216.9 0.6 copy.46
  (1 shorter events, 0.0 us)
Async XLA Ops:
  208.2 2.0 copy-start
  210.2 1.0 copy-start.8
  210.2 1.6 copy-start.3
  211.8 0.8 copy-start.7
  211.8 1.4 copy-start.6
  212.5 1.2 copy-start.4
  213.2 2.0 copy-start.2
  213.8 0.8 copy-start.5
  215.2 1.0 copy-start.1
  216.1 0.7 copy-start.9
